TPU v7x, 128 devices: a whole 4x4x4 slice. The times are simulated.
128 devices in a mesh: section: 2 (over core), fsdp: 4 (over x), ctx: 16 (over y, z).
Axes of the slice: x: 4, y: 4, z: 4, core: 2. Of those that a mesh axis runs over, the one named last changes fastest.
Arguments:
- boundary: bfloat16 [2, 2, 4, 1024, 768], P('section', None, 'fsdp', 'ctx'), may hold values from -6 to 6
- block_order: int32 [32], replicated, may hold values from 0 to 31, each once
- qkv_weight: bfloat16 [2, 768, 2304], P('section', ('fsdp', 'ctx')), may hold values from -0.21875 to 0.21875
- out_weight: bfloat16 [2, 768, 768], P('section', ('fsdp', 'ctx')), may hold values from -2.5 to 2.5
- fc_weight: bfloat16 [2, 768, 3072], P('section', ('fsdp', 'ctx')), may hold values from -0.21875 to 0.21875
- proj_weight: bfloat16 [2, 3072, 768], P('section', ('fsdp', 'ctx')), may hold values from -0.109375 to 0.109375
- gains: bfloat16 [2, 2, 768], P('section', None, ('fsdp', 'ctx')), may hold values from 0.099609375 to 1.8984375
- biases: bfloat16 [2, 6, 768], P('section', None, ('fsdp', 'ctx')), may hold values from -3 to 3
- fc_bias: bfloat16 [2, 3072], P('section', ('fsdp', 'ctx')), may hold values from -3 to 3
Outputs:
- ends: float32 [2, 2, 4, 1024, 768], P('section', None, 'fsdp', 'ctx')
- qkv_grad: float32 [2, 768, 2304], P('section', ('fsdp', 'ctx'))
- out_grad: float32 [2, 768, 768], P('section', ('fsdp', 'ctx'))
- fc_grad: float32 [2, 768, 3072], P('section', ('fsdp', 'ctx'))
- proj_grad: float32 [2, 3072, 768], P('section', ('fsdp', 'ctx'))
- gains_grad: float32 [2, 2, 768], P('section', None, ('fsdp', 'ctx'))
- biases_grad: float32 [2, 6, 768], P('section', None, ('fsdp', 'ctx'))
- fc_bias_grad: float32 [2, 3072], P('section', ('fsdp', 'ctx'))
Inputs may be any that keep to these rules, and one draw needn't show every extreme that they name: `block_order`: a permutation of the 32 block numbers, the same for every sequence.
All inputs are finite; a program needn't handle non-finite values.
Results may differ from a plain program's by a relative error of at most 0.014.
Values may be sent and summed in bfloat16 or wider, within the bound.
A program may use at most 192 MiB of HBM per device.

v0:
```python
import jax
import jax.numpy as jnp
from jax import lax
from jax.sharding import PartitionSpec as P

HEADS = 12
HD = 64
FF = 3072


EPS = 1e-05
ROOT = 0.7978845608028654
CUBIC = 0.044715


def passed_along(shard, axis, by):
    devices = lax.axis_size(axis)
    pairs = [(i, i + by) for i in range(devices) if 0 <= i + by < devices]
    return lax.ppermute(shard, axis, pairs)


def layer_norm(values, gain, shift):
    centre = values - jnp.mean(values, -1, keepdims=True)
    spread = jnp.mean(centre * centre, -1, keepdims=True)
    return centre * lax.rsqrt(spread + EPS) * gain + shift


def gelu_tanh(values):
    return 0.5 * values * (1.0 + jnp.tanh(ROOT * (values + CUBIC * values * values * values)))


def positions(block_order, seq_len, block_len):
    index = jnp.arange(seq_len, dtype=jnp.int32)
    which = index // block_len
    table = jnp.arange(block_order.shape[0], dtype=jnp.int32)
    chosen = jnp.sum(jnp.where(which[:, None] == table[None, :], block_order[None, :], 0), axis=1)
    return chosen * block_len + index % block_len


def collect(qkv_weight, out_weight, fc_weight, proj_weight, gains, biases, fc_bias):
    return (
        lax.all_gather(qkv_weight[0], ("fsdp", "ctx"), axis=0, tiled=True),
        lax.all_gather(out_weight[0], ("fsdp", "ctx"), axis=0, tiled=True),
        lax.all_gather(fc_weight[0], ("fsdp", "ctx"), axis=0, tiled=True),
        lax.all_gather(proj_weight[0], ("fsdp", "ctx"), axis=0, tiled=True),
        lax.all_gather(gains[0], ("fsdp", "ctx"), axis=1, tiled=True),
        lax.all_gather(biases[0], ("fsdp", "ctx"), axis=1, tiled=True),
        lax.all_gather(fc_bias[0], ("fsdp", "ctx"), axis=0, tiled=True),
    )


def split_heads(rows):
    return rows.reshape(rows.shape[0], rows.shape[1], HEADS, HD)


def join_heads(rows):
    return rows.reshape(rows.shape[0], rows.shape[1], HEADS * HD)


def attend(queries, all_keys, all_values, allowed):
    score_scale = HD ** (-0.5)
    raw_scores = jnp.einsum(
        "sqhd,skhd->shqk",
        split_heads(queries),
        split_heads(all_keys),
        preferred_element_type=jnp.float32,
    )
    scores = jnp.where(allowed[None, None], raw_scores * score_scale, -1e30)
    row_top = jnp.max(scores, -1, keepdims=True)
    exponent = jnp.exp(scores - row_top)
    row_total = jnp.sum(exponent, -1, keepdims=True)
    soft = (exponent / row_total).astype(jnp.bfloat16)
    attention_output = jnp.einsum(
        "shqk,skhd->sqhd", soft, split_heads(all_values), preferred_element_type=jnp.float32
    )
    return (join_heads(attention_output), row_top + jnp.log(row_total))


def soft_terms(queries, key_rows, value_rows, grad_att, allowed, log_total, centre):
    score_scale = HD ** (-0.5)
    raw_scores = jnp.einsum(
        "sqhd,skhd->shqk",
        split_heads(queries),
        split_heads(key_rows),
        preferred_element_type=jnp.float32,
    )
    scores = jnp.where(allowed[None, None], raw_scores * score_scale, -1e30)
    soft = jnp.exp(scores - log_total)
    grad_soft = jnp.einsum(
        "sqhd,skhd->shqk",
        split_heads(grad_att),
        split_heads(value_rows),
        preferred_element_type=jnp.float32,
    )
    centre = jnp.sum(soft * grad_soft, -1, keepdims=True)
    grad_scores = (score_scale * soft * (grad_soft - centre)).astype(jnp.bfloat16)
    return (soft, grad_scores, centre)


def key_side(soft, grad_scores, queries, grad_att):
    part_keys = jnp.einsum(
        "shqk,sqhd->skhd", grad_scores, split_heads(queries), preferred_element_type=jnp.float32
    )
    part_values = jnp.einsum(
        "shqk,sqhd->skhd",
        soft.astype(jnp.bfloat16),
        split_heads(grad_att),
        preferred_element_type=jnp.float32,
    )
    return (join_heads(part_keys), join_heads(part_values))


def forward(weights_held, inputs, allowed):
    query_key_value_weight, output_weight, w_fc, w_proj, gain_rows, bias_rows, fc_shift = (
        weights_held
    )
    gains_full = gain_rows.astype(jnp.float32)
    bias_full = bias_rows.astype(jnp.float32)
    width = output_weight.shape[0]
    normalized_input = layer_norm(inputs, gains_full[0], bias_full[0]).astype(jnp.bfloat16)
    projected_output = jnp.einsum(
        "vzq,qj->vzj", normalized_input, query_key_value_weight, preferred_element_type=jnp.float32
    )
    queries = (projected_output[..., :width] + bias_full[1]).astype(jnp.bfloat16)
    key_rows = projected_output[..., width : 2 * width].astype(jnp.bfloat16)
    value_rows = (projected_output[..., 2 * width :] + bias_full[2]).astype(jnp.bfloat16)
    all_keys, all_values = (
        lax.all_gather(key_rows, "ctx", axis=1, tiled=True),
        lax.all_gather(value_rows, "ctx", axis=1, tiled=True),
    )
    attended_full, log_total = attend(queries, all_keys, all_values, allowed)
    attention_output = attended_full.astype(jnp.bfloat16)
    resid = inputs + (
        jnp.einsum(
            "vzq,qj->vzj", attention_output, output_weight, preferred_element_type=jnp.float32
        )
        + bias_full[3]
    )
    second = layer_norm(resid, gains_full[1], bias_full[4]).astype(jnp.bfloat16)
    pre_act = jnp.einsum(
        "snd,df->snf", second, w_fc, preferred_element_type=jnp.float32
    ) + fc_shift.astype(jnp.float32)
    activ = gelu_tanh(pre_act).astype(jnp.bfloat16)
    output = resid + (
        jnp.einsum("snf,fd->snd", activ, w_proj, preferred_element_type=jnp.float32) + bias_full[5]
    )
    saved = (
        inputs,
        normalized_input,
        queries,
        key_rows,
        value_rows,
        log_total,
        attention_output,
        resid,
        second,
        pre_act,
        activ,
    )
    return (saved, all_keys, all_values, output)


def backward(weights_held, saved, grad_out, allowed, all_keys, all_values, accum):
    query_key_value_weight, output_weight, w_fc, w_proj, gain_rows, bias_rows, fc_shift = (
        weights_held
    )
    (
        inputs,
        normalized_input,
        queries,
        key_rows,
        value_rows,
        log_total,
        attention_output,
        resid,
        second,
        pre_act,
        activ,
    ) = saved
    gains_full = gain_rows.astype(jnp.float32)
    bias_full = bias_rows.astype(jnp.float32)
    grad_mlp = grad_out.astype(jnp.bfloat16)
    grad_proj = jnp.einsum("snf,snd->fd", activ, grad_mlp, preferred_element_type=jnp.float32)
    grad_proj_bias = jnp.sum(grad_mlp.astype(jnp.float32), (0, 1))
    grad_act = jnp.einsum("snd,fd->snf", grad_mlp, w_proj, preferred_element_type=jnp.float32)
    unused_act, gelu_pull = jax.vjp(gelu_tanh, pre_act)
    grad_pre = gelu_pull(grad_act)[0].astype(jnp.bfloat16)
    grad_fc = jnp.einsum("snd,snf->df", second, grad_pre, preferred_element_type=jnp.float32)
    grad_fc_bias = jnp.sum(grad_pre.astype(jnp.float32), (0, 1))
    grad_second = jnp.einsum("snf,df->snd", grad_pre, w_fc, preferred_element_type=jnp.float32)
    unused_second, second_pull = jax.vjp(layer_norm, resid, gains_full[1], bias_full[4])
    grad_resid_norm, grad_gain_two, grad_shift_two = second_pull(grad_second)
    grad_resid = grad_out + grad_resid_norm
    branch_gradient = grad_resid.astype(jnp.bfloat16)
    grad_out_weight = jnp.einsum(
        "kvp,kvm->pm", attention_output, branch_gradient, preferred_element_type=jnp.float32
    )
    grad_out_bias = jnp.sum(branch_gradient.astype(jnp.float32), (0, 1))
    grad_att = jnp.einsum(
        "zjh,ih->zji", branch_gradient, output_weight, preferred_element_type=jnp.float32
    ).astype(jnp.bfloat16)
    soft, grad_scores, centre = soft_terms(
        queries, all_keys, all_values, grad_att, allowed, log_total, None
    )
    grad_query = join_heads(
        jnp.einsum(
            "shqk,skhd->sqhd",
            grad_scores,
            split_heads(all_keys),
            preferred_element_type=jnp.float32,
        )
    )
    part_keys, part_values = key_side(soft, grad_scores, queries, grad_att)
    grad_keys, grad_values = (
        lax.psum_scatter(
            part_keys.astype(jnp.bfloat16), "ctx", scatter_dimension=1, tiled=True
        ).astype(jnp.float32),
        lax.psum_scatter(
            part_values.astype(jnp.bfloat16), "ctx", scatter_dimension=1, tiled=True
        ).astype(jnp.float32),
    )
    query_low = grad_query.astype(jnp.bfloat16)
    value_low = grad_values.astype(jnp.bfloat16)
    mixed_gradient = jnp.concatenate([query_low, grad_keys.astype(jnp.bfloat16), value_low], -1)
    query_key_value_gradient = jnp.einsum(
        "kvp,kvm->pm", normalized_input, mixed_gradient, preferred_element_type=jnp.float32
    )
    grad_query_bias = jnp.sum(query_low.astype(jnp.float32), (0, 1))
    grad_value_bias = jnp.sum(value_low.astype(jnp.float32), (0, 1))
    normalized_gradient = jnp.einsum(
        "zjh,ih->zji", mixed_gradient, query_key_value_weight, preferred_element_type=jnp.float32
    )
    unused_first, first_pull = jax.vjp(layer_norm, inputs, gains_full[0], bias_full[0])
    grad_in_norm, grad_gain_one, grad_shift_one = first_pull(normalized_gradient)
    grad_in = grad_resid + grad_in_norm
    updated = (
        accum[0] + query_key_value_gradient,
        accum[1] + grad_out_weight,
        accum[2] + grad_fc,
        accum[3] + grad_proj,
        accum[4] + jnp.stack([grad_gain_one, grad_gain_two]),
        accum[5]
        + jnp.stack(
            [
                grad_shift_one,
                grad_query_bias,
                grad_value_bias,
                grad_out_bias,
                grad_shift_two,
                grad_proj_bias,
            ]
        ),
        accum[6] + grad_fc_bias,
    )
    return (updated, grad_in)


def local(
    boundary, block_order, qkv_weight, out_weight, fc_weight, proj_weight, gains, biases, fc_bias
):
    section_index = lax.axis_index("section")
    local_len = boundary.shape[3]
    seq_len = local_len * lax.axis_size("ctx")
    micro_count = boundary.shape[1]
    width = boundary.shape[4]
    block_len = seq_len // block_order.shape[0]
    key_pos = positions(block_order, seq_len, block_len)
    query_pos = lax.dynamic_slice_in_dim(key_pos, lax.axis_index("ctx") * local_len, local_len)
    allowed = key_pos[None, :] <= query_pos[:, None]
    stored = collect(qkv_weight, out_weight, fc_weight, proj_weight, gains, biases, fc_bias)

    def fetch_weights():
        return stored

    saved_steps = []
    key_steps = []
    out_steps = []
    incoming = jnp.zeros(boundary.shape[2:], jnp.bfloat16)
    for moment in range(micro_count + 1):
        own_rows = boundary[0, min(moment, micro_count - 1)]
        inputs = jnp.where(section_index == 0, own_rows, incoming).astype(jnp.float32)
        saved, all_keys, all_values, output = forward(fetch_weights(), inputs, allowed)
        saved_steps.append(saved)
        key_steps.append((all_keys, all_values))
        out_steps.append(output)
        if moment < micro_count:
            incoming = passed_along(output.astype(jnp.bfloat16), "section", 1)
    accum = (
        jnp.zeros((width, 3 * width), jnp.float32),
        jnp.zeros((width, width), jnp.float32),
        jnp.zeros((width, FF), jnp.float32),
        jnp.zeros((FF, width), jnp.float32),
        jnp.zeros((2, width), jnp.float32),
        jnp.zeros((6, width), jnp.float32),
        jnp.zeros((FF,), jnp.float32),
    )
    returned = jnp.zeros(boundary.shape[2:], jnp.bfloat16)
    grad_steps = []
    for moment in range(micro_count + 1):
        top_rows = boundary[0, max(micro_count - 1 - moment, 0)].astype(jnp.float32)
        if moment == micro_count:
            top_rows = jnp.zeros_like(top_rows)
        grad_out = jnp.where(section_index == 1, top_rows, returned.astype(jnp.float32))
        saved = saved_steps[micro_count - moment]
        all_keys, all_values = (
            lax.all_gather(saved[3], "ctx", axis=1, tiled=True),
            lax.all_gather(saved[4], "ctx", axis=1, tiled=True),
        )
        accum, grad_in = backward(
            fetch_weights(), saved, grad_out, allowed, all_keys, all_values, accum
        )
        grad_steps.append(grad_in)
        if moment < micro_count:
            returned = passed_along(grad_in.astype(jnp.bfloat16), "section", -1)
    ends = jnp.stack(
        [
            jnp.where(section_index == 0, grad_steps[micro_count - member], out_steps[member + 1])
            for member in range(micro_count)
        ]
    )
    shares = (
        lax.psum_scatter(accum[0], ("fsdp", "ctx"), scatter_dimension=0, tiled=True),
        lax.psum_scatter(accum[1], ("fsdp", "ctx"), scatter_dimension=0, tiled=True),
        lax.psum_scatter(accum[2], ("fsdp", "ctx"), scatter_dimension=0, tiled=True),
        lax.psum_scatter(accum[3], ("fsdp", "ctx"), scatter_dimension=0, tiled=True),
        lax.psum_scatter(accum[4], ("fsdp", "ctx"), scatter_dimension=1, tiled=True),
        lax.psum_scatter(accum[5], ("fsdp", "ctx"), scatter_dimension=1, tiled=True),
        lax.psum_scatter(accum[6], ("fsdp", "ctx"), scatter_dimension=0, tiled=True),
    )
    return (
        ends[None],
        shares[0][None],
        shares[1][None],
        shares[2][None],
        shares[3][None],
        shares[4][None],
        shares[5][None],
        shares[6][None],
    )


def solution(mesh):
    in_specs = (
        P("section", None, "fsdp", "ctx", None),
        P(),
        P("section", ("fsdp", "ctx"), None),
        P("section", ("fsdp", "ctx"), None),
        P("section", ("fsdp", "ctx"), None),
        P("section", ("fsdp", "ctx"), None),
        P("section", None, ("fsdp", "ctx")),
        P("section", None, ("fsdp", "ctx")),
        P("section", ("fsdp", "ctx")),
    )
    out_specs = (
        P("section", None, "fsdp", "ctx", None),
        P("section", ("fsdp", "ctx"), None),
        P("section", ("fsdp", "ctx"), None),
        P("section", ("fsdp", "ctx"), None),
        P("section", ("fsdp", "ctx"), None),
        P("section", None, ("fsdp", "ctx")),
        P("section", None, ("fsdp", "ctx")),
        P("section", ("fsdp", "ctx")),
    )
    return jax.shard_map(local, mesh=mesh, in_specs=in_specs, out_specs=out_specs, check_vma=False)
```

profile of v0, /device:TPU:0, one launch (start us, length us, event | category | flops | bytes accessed | tf_op | source)
XLA Modules:
  0.0 2207.2 jit_solution(2857342876651905748)
XLA Ops:
  13.7 180.8 %all-gather.1 = bf16[1,6,768]{1,0,2:T(2,128)(2,1)S(1)} all-gather(bf16[1,6,12]{1,0,2:T(2,128)(2,1)S(1)} %copy.153), channel_id=3, replica_groups=mesh['section'=2,'fsdp'=4,'ctx'=16] {'fsdp','ctx'}, dimensions={2}, use_global_device_ids=true | all-gather | bytes 9360 | tf_op jit(solution)/shard_map/all_gather | solution.py:47
  194.9 172.0 %all-gather = bf16[1,2,768]{1,0,2:T(2,128)(2,1)S(1)} all-gather(bf16[1,2,12]{1,0,2:T(2,128)(2,1)S(1)} %copy.152), channel_id=2, replica_groups=mesh['section'=2,'fsdp'=4,'ctx'=16] {'fsdp','ctx'}, dimensions={2}, use_global_device_ids=true | all-gather | bytes 3120 | tf_op jit(solution)/shard_map/all_gather | solution.py:46
  368.2 4.6 slice_reduce_fusion.2
  373.3 13.5 slice_reduce_fusion.1
  386.8 3.6 copy.193
  399.5 177.5 %all-reduce = bf16[3072]{0:T(1024)(128)(2,1)} all-reduce(bf16[3072]{0:T(1024)(128)(2,1)} %dynamic-update-slice), channel_id=7, replica_groups=mesh['section'=2,'fsdp'=4,'ctx'=16] {'fsdp','ctx'}, use_global_device_ids=true, to_apply=%add | all-reduce | flops 3072 | bytes 12288
  579.9 2.9 copy.194
  584.5 7.6 copy.195
  606.8 3.6 fusion.153
  617.9 35.9 %all-gather.24.cloned.1.call-done = bf16[1,1024,768]{2,1,0:T(8,128)(2,1)} async-done(((bf16[1,64,768]{2,1,0:T(8,128)(2,1)}), bf16[1,1024,768]{2,1,0:T(8,128)(2,1)}) %all-gather.24.cloned.1.call-update) | async-done | bytes 1572880 | tf_op jit(solution)/shard_map/all_gather | solution.py:128
  659.2 40.7 %all-gather.22.cloned.1.call-done = bf16[1,1024,768]{2,1,0:T(8,128)(2,1)} async-done(((bf16[1,64,768]{2,1,0:T(8,128)(2,1)}), bf16[1,1024,768]{2,1,0:T(8,128)(2,1)}) %all-gather.22.cloned.1.call-update) | async-done | bytes 1572880 | tf_op jit(solution)/shard_map/all_gather | solution.py:129
  701.8 3.3 fusion.85
  715.3 42.3 %all-gather.28.cloned.1.call-done = bf16[1,1024,768]{2,1,0:T(8,128)(2,1)} async-done(((bf16[1,64,768]{2,1,0:T(8,128)(2,1)}), bf16[1,1024,768]{2,1,0:T(8,128)(2,1)}) %all-gather.28.cloned.1.call-update) | async-done | bytes 1572880 | tf_op jit(solution)/shard_map/all_gather | solution.py:128
  762.6 41.0 %all-gather.26.cloned.1.call-done = bf16[1,1024,768]{2,1,0:T(8,128)(2,1)} async-done(((bf16[1,64,768]{2,1,0:T(8,128)(2,1)}), bf16[1,1024,768]{2,1,0:T(8,128)(2,1)}) %all-gather.26.cloned.1.call-update) | async-done | bytes 1572880 | tf_op jit(solution)/shard_map/all_gather | solution.py:129
  806.3 3.3 fusion.84
  818.5 3.7 convolution_convert_fusion.4
  831.7 3.2 convert_reduce_fusion.5
  837.5 60.6 %reduce-scatter.18.cloned.1.call-done = bf16[1,64,768]{2,1,0:T(8,128)(2,1)} async-done(((bf16[1,1024,768]{2,1,0:T(8,128)(2,1)}), bf16[1,64,768]{2,1,0:T(8,128)(2,1)}) %reduce-scatter.18.cloned.1.call-update) | async-done | bytes 98320 | tf_op jit(solution)/shard_map/reduce_scatter | solution.py:218
  898.1 76.0 %reduce-scatter.16.cloned.1.call-done = bf16[1,64,768]{2,1,0:T(8,128)(2,1)} async-done(((bf16[1,1024,768]{2,1,0:T(8,128)(2,1)}), bf16[1,64,768]{2,1,0:T(8,128)(2,1)}) %reduce-scatter.16.cloned.1.call-update) | async-done | bytes 98320 | tf_op jit(solution)/shard_map/reduce_scatter | solution.py:215
  983.9 4.7 convert_reduce_fusion.1
  995.7 3.8 convolution_convert_fusion.2
  1002.2 3.5 multiply_reduce_fusion.1
  1012.1 3.0 convert_reduce_fusion.4
  1017.8 58.1 %reduce-scatter.22.cloned.1.call-done = bf16[1,64,768]{2,1,0:T(8,128)(2,1)} async-done(((bf16[1,1024,768]{2,1,0:T(8,128)(2,1)}), bf16[1,64,768]{2,1,0:T(8,128)(2,1)}) %reduce-scatter.22.cloned.1.call-update) | async-done | bytes 98320 | tf_op jit(solution)/shard_map/reduce_scatter | solution.py:218
  1075.9 76.1 %reduce-scatter.20.cloned.1.call-done = bf16[1,64,768]{2,1,0:T(8,128)(2,1)} async-done(((bf16[1,1024,768]{2,1,0:T(8,128)(2,1)}), bf16[1,64,768]{2,1,0:T(8,128)(2,1)}) %reduce-scatter.20.cloned.1.call-update) | async-done | bytes 98320 | tf_op jit(solution)/shard_map/reduce_scatter | solution.py:215
  1152.0 3.0 fusion.203
  1161.1 4.6 convert_reduce_fusion
  1173.0 3.7 convolution_convert_fusion
  1179.4 3.5 multiply_reduce_fusion
  1193.7 5.2 add_add_fusion
  1211.6 6.1 fusion.308
  1224.7 5.1 fusion.235
  1240.7 6.2 fusion.311
  1253.9 4.4 fusion.150
  1258.4 4.1 fusion.234
  1272.4 4.5 add_add_fusion.3
  1276.9 11.7 add_add_fusion.1
  1288.6 40.0 %reduce-scatter.24.cloned.1.call-done = bf16[1,64,768]{2,1,0:T(8,128)(2,1)} async-done(((bf16[1,1024,768]{2,1,0:T(8,128)(2,1)}), bf16[1,64,768]{2,1,0:T(8,128)(2,1)}) %reduce-scatter.24.cloned.1.call-update) | async-done | bytes 98320 | tf_op jit(solution)/shard_map/reduce_scatter | solution.py:215
  1328.5 9.3 add_add_fusion.2
  1337.9 297.0 %fusion.315 = (f32[16,2304]{1,0:T(8,128)}, f32[16,768]{1,0:T(8,128)}, f32[16,3072]{1,0:T(8,128)}) fusion(f32[768,2304]{1,0:T(8,128)} %add_add_fusion.2, f32[768,768]{1,0:T(8,128)} %add_add_fusion.3, f32[768,3072]{1,0:T(8,128)} %add_add_fusion.1), kind=kCustom, calls=%all-reduce-scatter.3 | all-reduce-scatter fusion | flops 6291457 | bytes 19268096
  1639.4 3.9 collective-permute-start.32
  1643.4 3.2 collective-permute-start.31
  1651.8 4.0 collective-permute-start.30
  1655.8 7.5 collective-permute-start.29
  1665.0 4.2 collective-permute-start.27
  1672.2 4.7 collective-permute-start.25
  1680.8 3.8 collective-permute-start.18
  1689.9 3.4 collective-permute-start.20
  1694.7 4.1 collective-permute-start.17
  1701.5 3.4 collective-permute-start.14
  1705.0 7.3 collective-permute-start.13
  1714.7 6.8 collective-permute-done.16
  1724.4 9.7 collective-permute-start.9
  1737.6 4.3 collective-permute-start.6
  1743.5 3.1 collective-permute-start.4
  1748.8 343.7 %all-reduce.10 = (f32[2,768]{1,0:T(2,128)S(1)}, f32[6,768]{1,0:T(8,128)S(1)}, f32[3072]{0:T(1024)S(1)}) all-reduce(f32[2,768]{1,0:T(2,128)S(1)} %fusion.279, f32[6,768]{1,0:T(8,128)S(1)} %add_add_fusion.13, f32[3072]{0:T(1024)S(1)} %copy-done.138), channel_id=19, replica_groups=mesh['section'=2,'fsdp'=4,'ctx'=16] {'fsdp','ctx'}, use_global_device_ids=true, to_apply=%region_50.51.clone | all-reduce | flops 9216 | bytes 73728
  2102.1 13.0 collective-permute-start.45
  2118.6 4.4 collective-permute-start.42
  2126.6 6.6 concatenate.13
  2133.9 17.5 concatenate.12
  2151.5 3.4 collective-permute-start.40
  2157.0 4.3 collective-permute-start.38
  2163.3 3.7 collective-permute-start.36
  2169.5 29.9 %concatenate.14 = f32[268,3072]{1,0:T(8,128)S(1)} concatenate(f32[12,3072]{1,0:T(8,128)} %copy-done.85, f32[16,3072]{1,0:T(8,128)} %copy-done.86, f32[16,3072]{1,0:T(8,128)} %copy-done.87, f32[16,3072]{1,0:T(8,128)} %copy-done.88, f32[16,3072]{1,0:T(8,128)} %copy-done.89, f32[16,3072]{1,0:T(8,128)} %copy-done.90, f32[16,3072]{1,0:T(8,128)} %copy-done.91, f32[16,3072]{1,0:T(8,128)} %copy-done.92, ...), dimensions={0} | concatenate | bytes 6586368
  (703 shorter events, 252.7 us)
Async XLA Ops:
  7.2 379.6 %all-gather.30.cloned.1.call-start = ((), (), s32[]{:S(2)}) async-start(), calls=%async_computation.20 | async-start | bytes 7188480 | tf_op jit(solution)/shard_map/all_gather | solution.py:42
  8.9 571.0 %all-gather.32.cloned.1.call-start = ((), (), s32[]{:S(2)}) async-start(), calls=%async_computation.21 | async-start | bytes 2396160 | tf_op jit(solution)/shard_map/all_gather | solution.py:43
  10.4 574.1 %all-gather.34.cloned.1.call-start = ((), (), s32[]{:S(2)}) async-start(), calls=%async_computation.22 | async-start | bytes 9584640 | tf_op jit(solution)/shard_map/all_gather | solution.py:44
  12.1 580.0 %all-gather.18.cloned.1.call-start = ((), (), s32[]{:S(2)}) async-start(), calls=%async_computation.7 | async-start | bytes 1671168 | tf_op jit(solution)/shard_map/all_gather | solution.py:129
  393.1 201.6 %all-gather.20.cloned.1.call-start = ((), (), s32[]{:S(2)}) async-start(), calls=%async_computation.8 | async-start | bytes 1671168 | tf_op jit(solution)/shard_map/all_gather | solution.py:128
  394.8 212.0 %all-gather.36.cloned.1.call-start = ((), (), s32[]{:S(2)}) async-start(), calls=%async_computation.23 | async-start | bytes 4792320 | tf_op jit(solution)/shard_map/all_gather | solution.py:45
  395.3 258.4 %all-gather.24.cloned.1.call-start = ((), (), s32[]{:S(2)}) async-start(), calls=%async_computation.10 | async-start | bytes 1671168 | tf_op jit(solution)/shard_map/all_gather | solution.py:128
  615.9 84.0 %all-gather.22.cloned.1.call-start = ((), (), s32[]{:S(2)}) async-start(), calls=%async_computation.9 | async-start | bytes 1671168 | tf_op jit(solution)/shard_map/all_gather | solution.py:129
  617.7 139.9 %all-gather.28.cloned.1.call-start = ((), (), s32[]{:S(2)}) async-start(), calls=%async_computation.12 | async-start | bytes 1671168 | tf_op jit(solution)/shard_map/all_gather | solution.py:128
  714.1 89.5 %all-gather.26.cloned.1.call-start = ((), (), s32[]{:S(2)}) async-start(), calls=%async_computation.11 | async-start | bytes 1671168 | tf_op jit(solution)/shard_map/all_gather | solution.py:129
  714.9 183.2 %reduce-scatter.18.cloned.1.call-start = ((), (), s32[]{:S(2)}) async-start(), calls=%async_computation.14 | async-start | bytes 1671168 | tf_op jit(solution)/shard_map/reduce_scatter | solution.py:218
  825.0 149.2 %reduce-scatter.16.cloned.1.call-start = ((), (), s32[]{:S(2)}) async-start(), calls=%async_computation.13 | async-start | bytes 1671168 | tf_op jit(solution)/shard_map/reduce_scatter | solution.py:215
  831.7 244.2 %reduce-scatter.22.cloned.1.call-start = ((), (), s32[]{:S(2)}) async-start(), calls=%async_computation.16 | async-start | bytes 1671168 | tf_op jit(solution)/shard_map/reduce_scatter | solution.py:218
  1002.1 149.8 %reduce-scatter.20.cloned.1.call-start = ((), (), s32[]{:S(2)}) async-start(), calls=%async_computation.15 | async-start | bytes 1671168 | tf_op jit(solution)/shard_map/reduce_scatter | solution.py:215
  1012.1 276.5 %reduce-scatter.26.cloned.1.call-start = ((), (), s32[]{:S(2)}) async-start(), calls=%async_computation.18 | async-start | bytes 1671168 | tf_op jit(solution)/shard_map/reduce_scatter | solution.py:218
  1179.3 149.2 %reduce-scatter.24.cloned.1.call-start = ((), (), s32[]{:S(2)}) async-start(), calls=%async_computation.17 | async-start | bytes 1671168 | tf_op jit(solution)/shard_map/reduce_scatter | solution.py:215
  1189.2 1011.0 %reduce-scatter.28.cloned.1.call-start = ((), (), s32[]{:S(2)}) async-start(), calls=%async_computation.19 | async-start | bytes 9584640 | tf_op jit(solution)/shard_map/reduce_scatter | solution.py:325
  1635.9 19.9 collective-permute-start.34
  1637.3 26.1 %collective-permute-start.33 = (f32[16,768]{1,0:T(8,128)}, f32[16,768]{1,0:T(8,128)S(1)}, u32[]{:S(2)}, u32[]{:S(2)}) collective-permute-start(f32[16,768]{1,0:T(8,128)} %get-tuple-element.80), channel_id=1, source_target_pairs={{0,14},{1,15},{2,16},{3,17},{4,18},{5,19},{6,20},{7,21},{8,22},{9,... | collective-permute-start | bytes 147464
  1639.4 25.5 %collective-permute-start.32 = (f32[16,768]{1,0:T(8,128)}, f32[16,768]{1,0:T(8,128)S(1)}, u32[]{:S(2)}, u32[]{:S(2)}) collective-permute-start(f32[16,768]{1,0:T(8,128)} %get-tuple-element.80), channel_id=1, source_target_pairs={{0,13},{1,14},{2,15},{3,16},{4,17},{5,18},{6,19},{7,20},{8,21},{9,... | collective-permute-start | bytes 147464
  1643.4 26.1 %collective-permute-start.31 = (f32[16,768]{1,0:T(8,128)}, f32[16,768]{1,0:T(8,128)S(1)}, u32[]{:S(2)}, u32[]{:S(2)}) collective-permute-start(f32[16,768]{1,0:T(8,128)} %get-tuple-element.80), channel_id=1, source_target_pairs={{0,12},{1,13},{2,14},{3,15},{4,16},{5,17},{6,18},{7,19},{8,20},{9,... | collective-permute-start | bytes 147464
  1651.8 20.4 collective-permute-start.30
  1655.8 21.1 collective-permute-start.29
  1663.4 14.9 collective-permute-start.28
  1665.0 15.8 collective-permute-start.27
  1669.5 16.1 collective-permute-start.26
  1672.2 16.0 collective-permute-start.25
  1677.0 12.9 collective-permute-start.24
  1678.3 15.0 collective-permute-start.23
  1680.8 24.1 %collective-permute-start.18 = (f32[16,2304]{1,0:T(8,128)}, f32[16,2304]{1,0:T(8,128)S(1)}, u32[]{:S(2)}, u32[]{:S(2)}) collective-permute-start(f32[16,2304]{1,0:T(8,128)} %get-tuple-element.79), channel_id=1, source_target_pairs={{0,15},{1,16},{2,17},{3,18},{4,19},{5,20},{6,21},{7,22},{8,23},{9,... | collective-permute-start | bytes 442376
  1685.6 9.1 collective-permute-start.22
  1688.2 10.6 collective-permute-start.21
  1689.9 10.3 collective-permute-start.20
  1693.3 8.2 collective-permute-start.19
  1694.7 18.7 collective-permute-start.17
  1698.8 22.7 %collective-permute-start.16 = (f32[16,2304]{1,0:T(8,128)}, f32[16,2304]{1,0:T(8,128)S(1)}, u32[]{:S(2)}, u32[]{:S(2)}) collective-permute-start(f32[16,2304]{1,0:T(8,128)} %get-tuple-element.79), channel_id=1, source_target_pairs={{0,13},{1,14},{2,15},{3,16},{4,17},{5,18},{6,19},{7,20},{8,21},{9,... | collective-permute-start | bytes 442376
  1700.2 22.9 %collective-permute-start.15 = (f32[16,2304]{1,0:T(8,128)}, f32[16,2304]{1,0:T(8,128)S(1)}, u32[]{:S(2)}, u32[]{:S(2)}) collective-permute-start(f32[16,2304]{1,0:T(8,128)} %get-tuple-element.79), channel_id=1, source_target_pairs={{0,12},{1,13},{2,14},{3,15},{4,16},{5,17},{6,18},{7,19},{8,20},{9,... | collective-permute-start | bytes 442376
  1701.5 22.9 %collective-permute-start.14 = (f32[16,2304]{1,0:T(8,128)}, f32[16,2304]{1,0:T(8,128)S(1)}, u32[]{:S(2)}, u32[]{:S(2)}) collective-permute-start(f32[16,2304]{1,0:T(8,128)} %get-tuple-element.79), channel_id=1, source_target_pairs={{0,11},{1,12},{2,13},{3,14},{4,15},{5,16},{6,17},{7,18},{8,19},{9,... | collective-permute-start | bytes 442376
  1705.0 29.2 %collective-permute-start.13 = (f32[16,2304]{1,0:T(8,128)}, f32[16,2304]{1,0:T(8,128)S(1)}, u32[]{:S(2)}, u32[]{:S(2)}) collective-permute-start(f32[16,2304]{1,0:T(8,128)} %get-tuple-element.79), channel_id=1, source_target_pairs={{0,10},{1,11},{2,12},{3,13},{4,14},{5,15},{6,16},{7,17},{8,18},{9,... | collective-permute-start | bytes 442376
  1713.4 22.8 %collective-permute-start.12 = (f32[16,2304]{1,0:T(8,128)}, f32[16,2304]{1,0:T(8,128)S(1)}, u32[]{:S(2)}, u32[]{:S(2)}) collective-permute-start(f32[16,2304]{1,0:T(8,128)} %get-tuple-element.79), channel_id=1, source_target_pairs={{0,9},{1,10},{2,11},{3,12},{4,13},{5,14},{6,15},{7,16},{8,17},{9,1... | collective-permute-start | bytes 442376
  1721.5 16.0 collective-permute-start.11
  1723.1 18.8 collective-permute-start.10
  1724.4 19.1 collective-permute-start.9
  1734.1 12.5 collective-permute-start.8
  1736.2 356.9 %collective-permute-start.7 = (f32[16,2304]{1,0:T(8,128)}, f32[16,2304]{1,0:T(8,128)S(1)}, u32[]{:S(2)}, u32[]{:S(2)}) collective-permute-start(f32[16,2304]{1,0:T(8,128)} %get-tuple-element.79), channel_id=1, source_target_pairs={{0,4},{1,5},{2,6},{3,7},{4,8},{5,9},{6,10},{7,11},{8,12},{9,13},{1... | collective-permute-start | bytes 442376
  1737.6 356.9 %collective-permute-start.6 = (f32[16,2304]{1,0:T(8,128)}, f32[16,2304]{1,0:T(8,128)S(1)}, u32[]{:S(2)}, u32[]{:S(2)}) collective-permute-start(f32[16,2304]{1,0:T(8,128)} %get-tuple-element.79), channel_id=1, source_target_pairs={{0,3},{1,4},{2,5},{3,6},{4,7},{5,8},{6,9},{7,10},{8,11},{9,12},{10... | collective-permute-start | bytes 442376
  1741.9 353.9 %collective-permute-start.5 = (f32[16,2304]{1,0:T(8,128)}, f32[16,2304]{1,0:T(8,128)S(1)}, u32[]{:S(2)}, u32[]{:S(2)}) collective-permute-start(f32[16,2304]{1,0:T(8,128)} %get-tuple-element.79), channel_id=1, source_target_pairs={{0,2},{1,3},{2,4},{3,5},{4,6},{5,7},{6,8},{7,9},{8,10},{9,11},{10,... | collective-permute-start | bytes 442376
  1743.5 353.6 %collective-permute-start.4 = (f32[16,2304]{1,0:T(8,128)}, f32[16,2304]{1,0:T(8,128)S(1)}, u32[]{:S(2)}, u32[]{:S(2)}) collective-permute-start(f32[16,2304]{1,0:T(8,128)} %get-tuple-element.79), channel_id=1, source_target_pairs={{0,1},{1,2},{2,3},{3,4},{4,5},{5,6},{6,7},{7,8},{8,9},{9,10},{10,1... | collective-permute-start | bytes 442376
  1746.7 351.8 %collective-permute-start.51 = (f32[12,3072]{1,0:T(8,128)S(1)}, f32[12,3072]{1,0:T(8,128)S(1)}, u32[]{:S(2)}, u32[]{:S(2)}) collective-permute-start(f32[12,3072]{1,0:T(8,128)S(1)} %slice.137), channel_id=1, source_target_pairs={{0,16},{1,17},{2,18},{3,19},{4,20},{5,21},{6,22},{7,23},{8,24},{9,... | collective-permute-start | bytes 442376
  2093.2 9.0 collective-permute-start.50
  2094.5 20.6 collective-permute-start.49
  2095.8 20.6 collective-permute-start.48
  2097.1 21.4 collective-permute-start.47
  2098.5 24.5 %collective-permute-start.46 = (f32[16,3072]{1,0:T(8,128)}, f32[16,3072]{1,0:T(8,128)S(1)}, u32[]{:S(2)}, u32[]{:S(2)}) collective-permute-start(f32[16,3072]{1,0:T(8,128)} %get-tuple-element.81), channel_id=1, source_target_pairs={{0,11},{1,12},{2,13},{3,14},{4,15},{5,16},{6,17},{7,18},{8,19},{9,... | collective-permute-start | bytes 589832
  2102.1 49.3 %collective-permute-start.45 = (f32[16,3072]{1,0:T(8,128)}, f32[16,3072]{1,0:T(8,128)S(1)}, u32[]{:S(2)}, u32[]{:S(2)}) collective-permute-start(f32[16,3072]{1,0:T(8,128)} %get-tuple-element.81), channel_id=1, source_target_pairs={{0,10},{1,11},{2,12},{3,13},{4,14},{5,15},{6,16},{7,17},{8,18},{9,... | collective-permute-start | bytes 589832
  2115.1 39.7 %collective-permute-start.44 = (f32[16,3072]{1,0:T(8,128)}, f32[16,3072]{1,0:T(8,128)S(1)}, u32[]{:S(2)}, u32[]{:S(2)}) collective-permute-start(f32[16,3072]{1,0:T(8,128)} %get-tuple-element.81), channel_id=1, source_target_pairs={{0,9},{1,10},{2,11},{3,12},{4,13},{5,14},{6,15},{7,16},{8,17},{9,1... | collective-permute-start | bytes 589832
  2116.4 40.5 %collective-permute-start.43 = (f32[16,3072]{1,0:T(8,128)}, f32[16,3072]{1,0:T(8,128)S(1)}, u32[]{:S(2)}, u32[]{:S(2)}) collective-permute-start(f32[16,3072]{1,0:T(8,128)} %get-tuple-element.81), channel_id=1, source_target_pairs={{0,8},{1,9},{2,10},{3,11},{4,12},{5,13},{6,14},{7,15},{8,16},{9,17... | collective-permute-start | bytes 589832
  2118.6 42.8 %collective-permute-start.42 = (f32[16,3072]{1,0:T(8,128)}, f32[16,3072]{1,0:T(8,128)S(1)}, u32[]{:S(2)}, u32[]{:S(2)}) collective-permute-start(f32[16,3072]{1,0:T(8,128)} %get-tuple-element.81), channel_id=1, source_target_pairs={{0,7},{1,8},{2,9},{3,10},{4,11},{5,12},{6,13},{7,14},{8,15},{9,16}... | collective-permute-start | bytes 589832
  2123.0 40.2 %collective-permute-start.41 = (f32[16,3072]{1,0:T(8,128)}, f32[16,3072]{1,0:T(8,128)}, u32[]{:S(2)}, u32[]{:S(2)}) collective-permute-start(f32[16,3072]{1,0:T(8,128)} %get-tuple-element.81), channel_id=1, source_target_pairs={{0,6},{1,7},{2,8},{3,9},{4,10},{5,11},{6,12},{7,13},{8,14},{9,15},... | collective-permute-start | bytes 589832
  2151.5 16.3 collective-permute-start.40
  2154.9 12.9 collective-permute-start.39
  2157.0 10.8 collective-permute-start.38
  2161.4 6.4 collective-permute-start.37
  2163.3 6.2 collective-permute-start.36
  (198 other events, 4344.4 us)
Sparse Core Ops, SparseCore 0:
  11.4 77.3 all-gather.29
  92.3 65.5 all-gather.31
  161.3 80.1 all-gather.33
  393.2 39.1 all-gather.17
  435.0 43.6 all-gather.19
  481.3 69.2 all-gather.35
  616.1 37.6 all-gather.23
  656.5 43.3 all-gather.21
  714.2 43.3 all-gather.27
  760.2 43.3 all-gather.25
  825.1 72.9 reduce-scatter.17
  901.2 72.8 reduce-scatter.15
  1002.3 73.5 reduce-scatter.21
  1078.9 72.9 reduce-scatter.19
  1179.5 72.9 reduce-scatter.25
  1255.5 72.9 reduce-scatter.23
  1333.5 420.4 reduce-scatter.27
where the time goes:
time: 2230 us; the launch traced here: 2210 us
  blocking collectives  1170 us (52%)
  waiting for transfers between devices  482 us (22%)
  local copies, waits for them, and re-layouts  192 us (9%)
  matrix products  152 us (7%)
  starting transfers between devices  151 us (7%)
  other arithmetic  38.7 us (2%)
    unnamed x3, blocking collectives  818 us
    reduce_scatter x3, waiting for transfers between devices, backward(): lax.psum_scatter(part_keys.astype(jnp.bfloat16), 'ctx', scatter_dimension...  192 us
    all_gather x1, blocking collectives, collect(): lax.all_gather(biases[0], ('fsdp', 'ctx'), axis=1, tiled=True)  181 us
    all_gather x1, blocking collectives, collect(): lax.all_gather(gains[0], ('fsdp', 'ctx'), axis=1, tiled=True)  172 us
    unnamed x48, starting transfers between devices  144 us
    reduce_scatter x3, waiting for transfers between devices, backward(): lax.psum_scatter(part_values.astype(jnp.bfloat16), 'ctx', scatter_dimensi...  119 us
    unnamed x407, local copies, waits for them, and re-layouts  102 us
    all_gather x3, waiting for transfers between devices, forward(): lax.all_gather(value_rows, 'ctx', axis=1, tiled=True)  81.6 us
  transfers between devices with their start and end apart: 69, of which 16 were waited for; matrix products, arithmetic and copies ran while one was open for 26% of the time, Pallas kernels for 0%

commit v1 on v0

v1 whole, which is shorter than its diff:
```python
import functools
import jax, jax.numpy as jnp
from jax import lax
from jax.experimental import pallas as pl
from jax.experimental.pallas import tpu as pltpu
from jax.sharding import PartitionSpec as P

MESH = pl.DeviceIdType.MESH
ORDERS = ((0, 1, 2), (1, 2, 0), (2, 0, 1))


def coordinates():
    ctx = lax.axis_index("ctx")
    return (lax.axis_index("fsdp"), ctx // 4, lax.rem(ctx, 4))


def device_at(section, spot):
    return (section, spot[0], spot[1] * 4 + spot[2])


def shifted(spot, axis, by):
    moved = list(spot)
    moved[axis] = lax.rem(spot[axis] + by, 4)
    return tuple(moved)


def slab(order, stage, spot, value, half=None, rows=None):
    index = [None, None, None]
    for t in range(3):
        axis = order[t]
        if t < stage:
            index[axis] = pl.ds(0, 4)
        elif t == stage:
            index[axis] = value
        else:
            index[axis] = spot[axis]
    if half is None:
        return tuple(index)
    if stage == 0:
        cut = rows // 2 // 16 * 16
        return tuple(index) + (pl.ds(0, cut) if half == 0 else pl.ds(cut, rows - cut),)
    index[order[0]] = pl.ds(2 * half, 2)
    return tuple(index)


def gather_kernel(priority, a_ref, b_ref, c_ref, ga, gb, gc, local_sem, send_sem, recv_sem, turn_sem):
    section = lax.axis_index("section")
    spot = coordinates()
    ins, outs = (a_ref, b_ref, c_ref), (ga, gb, gc)
    barrier = pltpu.get_barrier_semaphore()
    for axis in range(3):
        for by in (1, 3):
            pl.semaphore_signal(barrier, inc=1, device_id=device_at(section, shifted(spot, axis, by)), device_id_type=MESH)
    if priority:
        pl.semaphore_signal(barrier, inc=1, device_id=device_at(1 - section, spot), device_id_type=MESH)
    pl.semaphore_wait(barrier, 7 if priority else 6)
    if priority:
        @pl.when(section == 1)
        def _():
            pl.semaphore_wait(turn_sem, 1)
    own = []
    for part in range(3):
        copy = pltpu.make_async_copy(ins[part], outs[part].at[spot], local_sem.at[part])
        copy.start()
        own.append(copy)

    def remote(part, src, dst, stage, way, by):
        order = ORDERS[part]
        return pltpu.make_async_remote_copy(
            src_ref=src, dst_ref=dst,
            send_sem=send_sem.at[part, stage, way], recv_sem=recv_sem.at[part, stage, way],
            device_id=device_at(section, shifted(spot, order[stage], by)), device_id_type=MESH)

    pending = []
    for stage in range(3):
        first = []
        for part in range(3):
            order = ORDERS[part]
            mine = spot[order[stage]]
            idx = slab(order, stage, spot, mine)
            src = ins[part] if stage == 0 else outs[part].at[idx]
            for way, by in ((0, 1), (1, 3)):
                copy = remote(part, src, outs[part].at[idx], stage, way, by)
                copy.start()
                pending.append(copy)
        if stage == 0:
            for copy in own:
                copy.wait()
        for part in range(3):
            order = ORDERS[part]
            rows = ins[part].shape[0]
            mine = spot[order[stage]]
            for way, by, back in ((0, 1, 3), (1, 3, 1)):
                came = lax.rem(mine + back, 4)
                idx = slab(order, stage, spot, came)
                remote(part, outs[part].at[idx], outs[part].at[idx], stage, way, by).wait_recv()
                idx = slab(order, stage, spot, came, way, rows)
                copy = remote(part, outs[part].at[idx], outs[part].at[idx], stage, way + 2, by)
                copy.start()
                pending.append(copy)
        for part in range(3):
            order = ORDERS[part]
            rows = ins[part].shape[0]
            far = lax.rem(spot[order[stage]] + 2, 4)
            for way, by in ((0, 1), (1, 3)):
                idx = slab(order, stage, spot, far, way, rows)
                remote(part, outs[part].at[idx], outs[part].at[idx], stage, way + 2, by).wait_recv()
    if priority:
        @pl.when(section == 0)
        def _():
            pl.semaphore_signal(turn_sem, inc=1, device_id=device_at(1, spot), device_id_type=MESH)
    for copy in pending:
        copy.wait_send()


def gather_all(a, b, c, priority=True):
    return pl.pallas_call(
        functools.partial(gather_kernel, priority),
        out_shape=[jax.ShapeDtypeStruct((4, 4, 4) + x.shape, x.dtype) for x in (a, b, c)],
        in_specs=[pl.BlockSpec(memory_space=pl.ANY)] * 3,
        out_specs=[pl.BlockSpec(memory_space=pl.ANY)] * 3,
        scratch_shapes=[
            pltpu.SemaphoreType.DMA((3,)),
            pltpu.SemaphoreType.DMA((3, 3, 4)),
            pltpu.SemaphoreType.DMA((3, 3, 4)),
            pltpu.SemaphoreType.REGULAR,
        ],
        compiler_params=pltpu.CompilerParams(collective_id=0, has_side_effects=True),
    )(a, b, c)


def half_of(ref, stage, half):
    if stage < 2:
        return ref.at[pl.ds(2 * half, 2)]
    rows = ref.shape[0]
    cut = rows // 2 // 16 * 16
    return ref.at[pl.ds(0, cut)] if half == 0 else ref.at[pl.ds(cut, rows - cut)]


def each_chunk(stage, half, rows, body):
    if stage == 0:
        lo, size = (0, 4) if half is None else (2 * half, 2)

        def step(i, carry):
            body((lo + i // 4, lax.rem(i, 4)))
            return carry

        lax.fori_loop(0, size * 4, step, 0)
    elif stage == 1:
        lo, size = (0, 4) if half is None else (2 * half, 2)

        def step(i, carry):
            body((lo + i,))
            return carry

        lax.fori_loop(0, size, step, 0)
    else:
        cut = rows // 2 // 16 * 16
        body((pl.ds(0, rows) if half is None else (pl.ds(0, cut) if half == 0 else pl.ds(cut, rows - cut)),))


def wide(ref, index):
    return ref[index].astype(jnp.float32)


def scatter_kernel(*refs):
    ins, outs = refs[:3], refs[3:6]
    inbox = refs[6:33]
    own, mid, work1, work2 = refs[33:36], refs[36:39], refs[39:42], refs[42:45]
    local_sem, send_sem, recv_sem = refs[45:48]
    section = lax.axis_index("section")
    spot = coordinates()
    barrier = pltpu.get_barrier_semaphore()
    for axis in range(3):
        for by in (1, 3):
            pl.semaphore_signal(barrier, inc=1, device_id=device_at(section, shifted(spot, axis, by)), device_id_type=MESH)
    pl.semaphore_wait(barrier, 6)

    def box(part, stage, which):
        return inbox[(part * 3 + stage) * 3 + which]

    def source(part, stage, value):
        axis = ORDERS[part][stage]
        if stage == 0:
            index = [pl.ds(0, 4)] * 3
            index[axis] = value
            return ins[part].at[tuple(index)]
        if stage == 1:
            return work1[part].at[:, value] if part == 1 else work1[part].at[value]
        return work2[part].at[value]

    def remote(part, stage, kind, way, src, dst):
        by = 1 if way == 0 else 3
        return pltpu.make_async_remote_copy(
            src_ref=src, dst_ref=dst,
            send_sem=send_sem.at[part, stage, 2 * kind + way], recv_sem=recv_sem.at[part, stage, 2 * kind + way],
            device_id=device_at(section, shifted(spot, ORDERS[part][stage], by)), device_id_type=MESH)

    pending = []
    loads = {}

    def place(part, stage):
        return spot[ORDERS[part][stage]]

    def start(part, stage):
        here = place(part, stage)
        far = source(part, stage, lax.rem(here + 2, 4))
        near = (source(part, stage, lax.rem(here + 1, 4)), source(part, stage, lax.rem(here + 3, 4)))
        for way in (0, 1):
            copy = remote(part, stage, 0, way, half_of(far, stage, way), half_of(box(part, stage, 0), stage, way))
            copy.start()
            pending.append(copy)
        for way in (0, 1):
            copy = remote(part, stage, 1, way, half_of(near[way], stage, 1 - way), half_of(box(part, stage, 1 + way), stage, 1 - way))
            copy.start()
            pending.append(copy)
        if stage == 0:
            copies = [pltpu.make_async_copy(half_of(near[way], 0, way), half_of(mid[part], 0, way), local_sem.at[part, way]) for way in (0, 1)]
            copies.append(pltpu.make_async_copy(source(part, 0, here), own[part], local_sem.at[part, 2]))
            for copy in copies:
                copy.start()
            loads[part] = copies

    def middle(part, stage):
        here = place(part, stage)
        rows = outs[part].shape[0]
        fwd = box(part, stage, 0)
        for way in (0, 1):
            got = half_of(fwd, stage, way)
            remote(part, stage, 0, way, got, got).wait_recv()
            if stage == 0:
                loads[part][way].wait()
                add = mid[part]
            else:
                add = source(part, stage, lax.rem(here + (1 if way == 0 else 3), 4))

            def body(index):
                fwd[index] = (wide(fwd, index) + wide(add, index)).astype(fwd.dtype)

            each_chunk(stage, way, rows, body)
            copy = remote(part, stage, 2, way, got, half_of(box(part, stage, 1 + way), stage, way))
            copy.start()
            pending.append(copy)

    def finish(part, stage):
        here = place(part, stage)
        rows = outs[part].shape[0]
        left, right = box(part, stage, 1), box(part, stage, 2)
        for way in (0, 1):
            got = half_of(box(part, stage, 1 + way), stage, 1 - way)
            remote(part, stage, 1, way, got, got).wait_recv()
            got = half_of(box(part, stage, 1 + way), stage, way)
            remote(part, stage, 2, way, got, got).wait_recv()
        if stage == 0:
            loads[part][2].wait()
            mine = own[part]
        else:
            mine = source(part, stage, here)
        into = (work1, work2, outs)[stage][part]

        def body(index):
            into[index] = (wide(mine, index) + wide(left, index) + wide(right, index)).astype(into.dtype)

        each_chunk(stage, None, rows, body)

    for part in range(3):
        start(part, 0)
    for stage in range(3):
        for part in range(3):
            middle(part, stage)
        for part in range(3):
            finish(part, stage)
            if stage < 2:
                start(part, stage + 1)
    for copy in pending:
        copy.wait_send()


def scatter_all(a, b, c):
    rows = [x.shape[3] for x in (a, b, c)]
    shapes = lambda r: ((4, 4, r, 768), (4, r, 768), (r, 768))
    scratch = []
    for r in rows:
        for s in range(3):
            scratch += [pltpu.VMEM(shapes(r)[s], jnp.bfloat16)] * 3
    for level in (0, 0, 0, 1):
        scratch += [pltpu.VMEM(shapes(r)[level], jnp.bfloat16) for r in rows]
    return pl.pallas_call(
        scatter_kernel,
        out_shape=[jax.ShapeDtypeStruct((r, 768), jnp.float32) for r in rows],
        in_specs=[pl.BlockSpec(memory_space=pl.ANY)] * 3,
        out_specs=[pl.BlockSpec(memory_space=pltpu.VMEM)] * 3,
        scratch_shapes=scratch + [
            pltpu.SemaphoreType.DMA((3, 3)),
            pltpu.SemaphoreType.DMA((3, 3, 6)),
            pltpu.SemaphoreType.DMA((3, 3, 6)),
        ],
        compiler_params=pltpu.CompilerParams(collective_id=1, has_side_effects=True, vmem_limit_bytes=56 * 2**20),
    )(a, b, c)


def to_heads_kernel(units, x_ref, y_ref, local_sem, send_sem, recv_sem):
    section, fsdp, me = lax.axis_index("section"), lax.axis_index("fsdp"), lax.axis_index("ctx")
    rows = x_ref.shape[2]
    barrier = pltpu.get_barrier_semaphore()

    def mine(at):
        return pl.ds(pl.multiple_of(at * rows, rows), rows)

    def remote(unit, sender):
        return pltpu.make_async_remote_copy(
            src_ref=x_ref.at[unit], dst_ref=y_ref.at[:, mine(sender)],
            send_sem=send_sem.at[unit], recv_sem=recv_sem.at[sender],
            device_id=(section, fsdp, unit), device_id_type=MESH)

    @pl.when(me < units)
    def _():
        for other in range(16):
            @pl.when(me != other)
            def _():
                pl.semaphore_signal(barrier, inc=1, device_id=(section, fsdp, other), device_id_type=MESH)
        pl.semaphore_wait(barrier, units - 1)

    @pl.when(me >= units)
    def _():
        pl.semaphore_wait(barrier, units)

    for unit in range(units):
        @pl.when(me != unit)
        def _():
            remote(unit, me).start()

        @pl.when(me == unit)
        def _():
            pltpu.make_async_copy(x_ref.at[unit], y_ref.at[:, mine(me)], local_sem).start()

    @pl.when(me < units)
    def _():
        pltpu.make_async_copy(x_ref.at[me], y_ref.at[:, mine(me)], local_sem).wait()
        for sender in range(16):
            @pl.when(me != sender)
            def _():
                remote(0, sender).wait_recv()

    for unit in range(units):
        @pl.when(me != unit)
        def _():
            remote(unit, me).wait_send()


def to_heads(x, ident):
    units, n, rows, lanes = x.shape
    return pl.pallas_call(
        functools.partial(to_heads_kernel, units),
        out_shape=jax.ShapeDtypeStruct((n, 16 * rows, lanes), x.dtype),
        in_specs=[pl.BlockSpec(memory_space=pl.ANY)],
        out_specs=pl.BlockSpec(memory_space=pl.ANY),
        scratch_shapes=[
            pltpu.SemaphoreType.DMA,
            pltpu.SemaphoreType.DMA((units,)),
            pltpu.SemaphoreType.DMA((16,)),
        ],
        compiler_params=pltpu.CompilerParams(collective_id=ident, has_side_effects=True),
    )(x)


def from_heads_kernel(units, y_ref, x_ref, local_sem, send_sem, recv_sem):
    section, fsdp, me = lax.axis_index("section"), lax.axis_index("fsdp"), lax.axis_index("ctx")
    rows = x_ref.shape[2]
    barrier = pltpu.get_barrier_semaphore()

    def mine(at):
        return pl.ds(pl.multiple_of(at * rows, rows), rows)

    def remote(unit, target):
        return pltpu.make_async_remote_copy(
            src_ref=y_ref.at[:, mine(target)], dst_ref=x_ref.at[unit],
            send_sem=send_sem.at[target], recv_sem=recv_sem.at[unit],
            device_id=(section, fsdp, target), device_id_type=MESH)

    for unit in range(units):
        @pl.when(me != unit)
        def _():
            pl.semaphore_signal(barrier, inc=1, device_id=(section, fsdp, unit), device_id_type=MESH)

    @pl.when(me < units)
    def _():
        pl.semaphore_wait(barrier, 15)
        for target in range(16):
            @pl.when(me != target)
            def _():
                remote(me, target).start()
        pltpu.make_async_copy(y_ref.at[:, mine(me)], x_ref.at[me], local_sem).start()
        pltpu.make_async_copy(y_ref.at[:, mine(me)], x_ref.at[me], local_sem).wait()

    for unit in range(units):
        @pl.when(me != unit)
        def _():
            remote(unit, 0).wait_recv()

    @pl.when(me < units)
    def _():
        for target in range(16):
            @pl.when(me != target)
            def _():
                remote(me, target).wait_send()


def from_heads(y, units, ident):
    n, total, lanes = y.shape
    return pl.pallas_call(
        functools.partial(from_heads_kernel, units),
        out_shape=jax.ShapeDtypeStruct((units, n, total // 16, lanes), y.dtype),
        in_specs=[pl.BlockSpec(memory_space=pl.ANY)],
        out_specs=pl.BlockSpec(memory_space=pl.ANY),
        scratch_shapes=[
            pltpu.SemaphoreType.DMA,
            pltpu.SemaphoreType.DMA((16,)),
            pltpu.SemaphoreType.DMA((units,)),
        ],
        compiler_params=pltpu.CompilerParams(collective_id=ident, has_side_effects=True),
    )(y)


EPS = 1e-05
ROOT = 0.7978845608028654
CUBIC = 0.044715
UNITS = 12
WIDTH = 768
PADDED = 1024
FF = 3072
ROWS = 128
HD = 64
BF = jnp.bfloat16
F32 = jnp.float32


def dot(left, right, over=((1,), (0,))):
    return lax.dot_general(left, right, (over, ((), ())), preferred_element_type=F32)


NT = ((1,), (1,))
TN = ((0,), (0,))


def ones_lane():
    return (lax.rem(lax.broadcasted_iota(jnp.int32, (1, PADDED), 1), 16) == 12).astype(F32)


def padded(rows, spread):
    return (dot(rows, spread) + ones_lane()).astype(BF)


def unpadded(rows, spread):
    high = rows.astype(BF)
    low = (rows - high.astype(F32)).astype(BF)
    return dot(high, spread, NT) + dot(low, spread, NT)


def extras(weight):
    lane = lax.rem(lax.broadcasted_iota(jnp.int32, (16, PADDED), 1), 16)
    row = lax.broadcasted_iota(jnp.int32, (16, PADDED), 0)
    return dot(((lane == row + 13) & (row < 3)).astype(F32).astype(BF), weight)


def normal(values):
    centre = values - jnp.mean(values, -1, keepdims=True)
    scale = lax.rsqrt(jnp.mean(centre * centre, -1, keepdims=True) + EPS)
    return centre * scale, scale


def norm_back(grad, n, scale):
    return scale * (grad - jnp.mean(grad, -1, keepdims=True) - n * jnp.mean(grad * n, -1, keepdims=True))


def flat(block):
    return block.reshape(PADDED, WIDTH)


def joined(ref):
    return jnp.concatenate(
        [jnp.concatenate([ref[m * 6 + h, 0] for h in range(6)], axis=1) for m in range(2)], axis=0)


def split_into(ref, rows):
    for m in range(2):
        for h in range(6):
            ref[m * 6 + h, 0] = rows[m * 64:(m + 1) * 64, h * 128:(h + 1) * 128]


def qkv_kernel(u_ref, w_ref, e_ref, x_ref, apad):
    weight = flat(w_ref[...])

    @pl.when(pl.program_id(0) == 0)
    def _():
        more = extras(weight)
        n, scale = normal(u_ref[...].astype(F32))
        apad[...] = padded((n * more[0:1] + more[1:2]).astype(BF), e_ref[...])

    split_into(x_ref, dot(apad[...], weight).astype(BF))


def whole(shape):
    return pl.BlockSpec(shape, lambda *i: (0,) * len(shape))


VMEM_LIMIT = 56 * 2**20


def qkv_call(u, ga, spread):
    return pl.pallas_call(
        qkv_kernel,
        grid=(3,),
        out_shape=jax.ShapeDtypeStruct((UNITS, 3, 64, 128), BF),
        in_specs=[whole((ROWS, WIDTH)), pl.BlockSpec((64, 16, WIDTH), lambda p: (0, p, 0)), whole((WIDTH, PADDED))],
        out_specs=pl.BlockSpec((UNITS, 1, 64, 128), lambda p: (0, p, 0, 0)),
        scratch_shapes=[pltpu.VMEM((ROWS, PADDED), BF)],
        compiler_params=pltpu.CompilerParams(vmem_limit_bytes=VMEM_LIMIT),
    )(u, ga, spread)


def gelu_parts(f):
    t = jnp.tanh(ROOT * (f + CUBIC * f * f * f))
    return t, 0.5 * f * (1.0 + t)


def mlp_kernel(o_ref, u_ref, wo_ref, wf_ref, wp_ref, e_ref, y_ref, r_ref, f_ref, bpad):
    @pl.when(pl.program_id(0) == 0)
    def _():
        wo = flat(wo_ref[...])
        more = extras(wo)
        r = u_ref[...].astype(F32) + dot(padded(joined(o_ref), e_ref[...]), wo)
        r_ref[...] = r
        n, scale = normal(r)
        bpad[...] = padded((n * more[0:1] + more[1:2]).astype(BF), e_ref[...])
        y_ref[...] = r + more[2:3]

    f = dot(bpad[...], flat(wf_ref[...]))
    f_ref[...] = f
    y_ref[...] += dot(gelu_parts(f)[1].astype(BF), wp_ref[...])


def mlp_call(o, u, ga, gb, gc, spread):
    piece = lambda p: pl.BlockSpec((64, 16, WIDTH), p)
    return pl.pallas_call(
        mlp_kernel,
        grid=(4,),
        out_shape=[
            jax.ShapeDtypeStruct((ROWS, WIDTH), F32),
            jax.ShapeDtypeStruct((ROWS, WIDTH), F32),
            jax.ShapeDtypeStruct((ROWS, FF), F32),
        ],
        in_specs=[
            whole((UNITS, 1, 64, 128)), whole((ROWS, WIDTH)), piece(lambda k: (0, 3, 0)),
            piece(lambda k: (0, k, 0)), pl.BlockSpec((WIDTH, WIDTH), lambda k: (k, 0)), whole((WIDTH, PADDED)),
        ],
        out_specs=[whole((ROWS, WIDTH)), whole((ROWS, WIDTH)), pl.BlockSpec((ROWS, WIDTH), lambda k: (0, k))],
        scratch_shapes=[pltpu.VMEM((ROWS, PADDED), BF)],
        compiler_params=pltpu.CompilerParams(vmem_limit_bytes=VMEM_LIMIT),
    )(o, u, ga, gb, gc, spread)


def mlp_back_kernel(full, g_ref, f_ref, r_ref, wo_ref, wf_ref, wp_ref, e_ref, *refs):
    if full:
        do_ref, dr_ref, small_ref, db_ref, dc_ref, bpad, dbacc = refs
    else:
        do_ref, dr_ref, dbacc = refs
    k = pl.program_id(0)

    @pl.when(k == 0)
    def _():
        dbacc[...] = jnp.zeros_like(dbacc)
        if full:
            more = extras(flat(wo_ref[...]))
            n, scale = normal(r_ref[...])
            bpad[...] = padded((n * more[0:1] + more[1:2]).astype(BF), e_ref[...])

    dm = g_ref[...]
    f = f_ref[...]
    t, act = gelu_parts(f)
    slope = 0.5 * (1.0 + t) + 0.5 * f * (1.0 - t * t) * (ROOT * (1.0 + 3 * CUBIC * f * f))
    df = (dot(dm, wp_ref[...], NT) * slope).astype(BF)
    if full:
        dc_ref[...] = dot(act.astype(BF), dm, TN).astype(BF)
        db_ref[...] = dot(bpad[...], df, TN).astype(BF).reshape(64, 16, WIDTH)
    dbacc[...] += dot(df, flat(wf_ref[...]), NT)

    @pl.when(k == 3)
    def _():
        wo = flat(wo_ref[...])
        more = extras(wo)
        n, scale = normal(r_ref[...])
        db = unpadded(dbacc[...], e_ref[...])
        dr = dm.astype(F32) + norm_back(more[0:1] * db, n, scale)
        dr_ref[...] = dr
        do = dot(dr.astype(BF), wo, NT).astype(BF)
        split_into(do_ref, dot(do, e_ref[...], NT).astype(BF))
        if full:
            small_ref[0:1] = jnp.sum(db * n, 0, keepdims=True)
            small_ref[1:2] = jnp.sum(db, 0, keepdims=True)
            small_ref[2:3] = jnp.sum(dm.astype(F32), 0, keepdims=True)
            small_ref[3:8] = jnp.zeros((5, WIDTH), F32)


def mlp_back_call(full, g, f, r, ga, gb, gc, spread):
    piece = lambda p: pl.BlockSpec((64, 16, WIDTH), p)
    out_shape = [jax.ShapeDtypeStruct((UNITS, 1, 64, 128), BF), jax.ShapeDtypeStruct((ROWS, WIDTH), F32)]
    out_specs = [whole((UNITS, 1, 64, 128)), whole((ROWS, WIDTH))]
    scratch = [pltpu.VMEM((ROWS, PADDED), F32)]
    if full:
        out_shape += [
            jax.ShapeDtypeStruct((8, WIDTH), F32),
            jax.ShapeDtypeStruct((64, 64, WIDTH), BF),
            jax.ShapeDtypeStruct((FF, WIDTH), BF),
        ]
        out_specs += [whole((8, WIDTH)), piece(lambda k: (0, k, 0)), pl.BlockSpec((WIDTH, WIDTH), lambda k: (k, 0))]
        scratch = [pltpu.VMEM((ROWS, PADDED), BF)] + scratch
    return pl.pallas_call(
        functools.partial(mlp_back_kernel, full),
        grid=(4,),
        out_shape=out_shape,
        in_specs=[
            whole((ROWS, WIDTH)), pl.BlockSpec((ROWS, WIDTH), lambda k: (0, k)), whole((ROWS, WIDTH)),
            piece(lambda k: (0, 3, 0)), piece(lambda k: (0, k, 0)),
            pl.BlockSpec((WIDTH, WIDTH), lambda k: (k, 0)), whole((WIDTH, PADDED)),
        ],
        out_specs=out_specs,
        scratch_shapes=scratch,
        compiler_params=pltpu.CompilerParams(vmem_limit_bytes=VMEM_LIMIT),
    )(g, f, r, ga, gb, gc, spread)


def qkv_back_kernel(full, dx_ref, w_ref, u_ref, dr_ref, e_ref, *refs):
    if full:
        o_ref, small_ref, gu_ref, da_ref, gain, daacc, apad = refs
    else:
        gu_ref, gain, daacc = refs
    p = pl.program_id(0)

    @pl.when(p == 0)
    def _():
        more = extras(flat(w_ref[...]))
        gain[...] = jnp.broadcast_to(more[0:1], gain.shape)
        daacc[...] = jnp.zeros_like(daacc)
        if full:
            n, scale = normal(u_ref[...].astype(F32))
            apad[...] = padded((n * more[0:1] + more[1:2]).astype(BF), e_ref[...])

    def stored(grad, rows):
        grad = grad.reshape(64, 16, WIDTH)
        if rows is not None:
            at = lax.broadcasted_iota(jnp.int32, (16, WIDTH), 0)
            add = jnp.zeros((16, WIDTH), F32)
            for i, row in enumerate(rows):
                add = add + jnp.where(at == 13 + i, row, 0.0)
            grad = grad + add[None]
        da_ref[...] = grad.astype(BF)

    @pl.when(p < 3)
    def _():
        dx = joined(dx_ref)
        daacc[...] += dot(dx, flat(w_ref[...]), NT)
        if full:
            grad = dot(apad[...], dx, TN)

            @pl.when(p == 0)
            def _():
                stored(grad, [small_ref[i:i + 1] for i in range(3)])

            @pl.when(p > 0)
            def _():
                stored(grad, None)

    @pl.when(p == (3 if full else 2))
    def _():
        n, scale = normal(u_ref[...].astype(F32))
        da = unpadded(daacc[...], e_ref[...])
        gu_ref[...] = dr_ref[...] + norm_back(gain[0:1] * da, n, scale)
        if full:
            grad = dot(padded(joined(o_ref), e_ref[...]), dr_ref[...].astype(BF), TN)
            stored(grad, [jnp.sum(da * n, 0, keepdims=True), jnp.sum(da, 0, keepdims=True)])


def qkv_back_call(full, dx, ga, u, dr, spread, o=None, small=None):
    last = lambda p: jnp.minimum(p, 2)
    in_specs = [
        pl.BlockSpec((UNITS, 1, 64, 128), lambda p: (0, last(p), 0, 0)),
        pl.BlockSpec((64, 16, WIDTH), lambda p: (0, last(p), 0)),
        whole((ROWS, WIDTH)), whole((ROWS, WIDTH)), whole((WIDTH, PADDED)),
    ]
    args = [dx, ga, u, dr, spread]
    out_shape = [jax.ShapeDtypeStruct((ROWS, WIDTH), F32)]
    out_specs = [whole((ROWS, WIDTH))]
    scratch = [pltpu.VMEM((8, WIDTH), F32), pltpu.VMEM((ROWS, PADDED), F32)]
    if full:
        in_specs += [whole((UNITS, 1, 64, 128)), whole((8, WIDTH))]
        args += [o, small]
        out_shape += [jax.ShapeDtypeStruct((64, 64, WIDTH), BF)]
        out_specs += [pl.BlockSpec((64, 16, WIDTH), lambda p: (0, p, 0))]
        scratch += [pltpu.VMEM((ROWS, PADDED), BF)]
    return pl.pallas_call(
        functools.partial(qkv_back_kernel, full),
        grid=(4 if full else 3,),
        out_shape=out_shape, in_specs=in_specs, out_specs=out_specs, scratch_shapes=scratch,
        compiler_params=pltpu.CompilerParams(vmem_limit_bytes=VMEM_LIMIT),
    )(*args)


SEQ = 1024
QB = 256


def head_mask(rows, head):
    lane = lax.broadcasted_iota(jnp.int32, rows.shape, 1)
    return jnp.where((lane >= 64 * head) & (lane < 64 * head + 64), rows, jnp.zeros_like(rows))


def scores_of(keys, query, kpos_ref, qpos):
    raw = dot(keys, query, NT)
    return jnp.where(kpos_ref[...] <= qpos, raw, -1e30)


def attend_kernel(x_ref, kpos_ref, qpos_ref, q_ref, o_ref, lse_ref, vt):
    @pl.when(pl.program_id(0) == 0)
    def _():
        vt[...] = x_ref[2].astype(F32).T.astype(BF)

    keys = x_ref[1]
    qpos = qpos_ref[...]
    query = q_ref[0] * jnp.array(0.125, BF)
    parts, stats = [], []
    for head in range(2):
        s = scores_of(keys, head_mask(query, head), kpos_ref, qpos)
        top = jnp.max(s, 0, keepdims=True)
        e = jnp.exp(s - top)
        total = jnp.sum(e, 0, keepdims=True)
        p = (e * (1.0 / total)).astype(BF)
        parts.append(dot(vt[64 * head:64 * head + 64], p))
        stats.append(top + jnp.log(total))
    o_ref[0] = jnp.concatenate(parts, 0).T.astype(BF)
    lse_ref[...] = jnp.concatenate(stats + [jnp.zeros((6, QB), F32)], 0)


def attend_call(x, kpos, qpos):
    return pl.pallas_call(
        attend_kernel,
        grid=(SEQ // QB,),
        out_shape=[jax.ShapeDtypeStruct((1, SEQ, 128), BF), jax.ShapeDtypeStruct((8, SEQ), F32)],
        in_specs=[
            whole((3, SEQ, 128)), whole((SEQ, 1)), pl.BlockSpec((1, QB), lambda i: (0, i)),
            pl.BlockSpec((1, QB, 128), lambda i: (0, i, 0)),
        ],
        out_specs=[pl.BlockSpec((1, QB, 128), lambda i: (0, i, 0)), pl.BlockSpec((8, QB), lambda i: (0, i))],
        scratch_shapes=[pltpu.VMEM((128, SEQ), BF)],
        compiler_params=pltpu.CompilerParams(vmem_limit_bytes=VMEM_LIMIT),
    )(x, kpos, qpos, x)


def attend_back_kernel(x_ref, kpos_ref, qpos_ref, q_ref, do_ref, lse_ref, out_ref, kt, dk, dv):
    i = pl.program_id(0)

    @pl.when(i == 0)
    def _():
        kt[...] = x_ref[1].astype(F32).T.astype(BF)
        dk[...] = jnp.zeros_like(dk)
        dv[...] = jnp.zeros_like(dv)

    keys, vals = x_ref[1], x_ref[2]
    qpos = qpos_ref[...]
    query, do = q_ref[0], do_ref[0]
    parts = []
    for head in range(2):
        q_own, do_own = head_mask(query, head), head_mask(do, head)
        s = scores_of(keys, q_own * jnp.array(0.125, BF), kpos_ref, qpos)
        p = jnp.exp(s - lse_ref[head:head + 1])
        dp = dot(vals, do_own, NT)
        delta = jnp.sum(p * dp, 0, keepdims=True)
        ds = (p * (dp - delta) * 0.125).astype(BF)
        dk[...] += dot(ds, q_own)
        dv[...] += dot(p.astype(BF), do_own)
        parts.append(dot(kt[64 * head:64 * head + 64], ds))
    at = pl.ds(pl.multiple_of(i * QB, QB), QB)
    out_ref[0, at] = jnp.concatenate(parts, 0).T.astype(BF)

    @pl.when(i == SEQ // QB - 1)
    def _():
        out_ref[1] = dk[...].astype(BF)
        out_ref[2] = dv[...].astype(BF)


def attend_back_call(x, kpos, qpos, do, lse):
    return pl.pallas_call(
        attend_back_kernel,
        grid=(SEQ // QB,),
        out_shape=jax.ShapeDtypeStruct((3, SEQ, 128), BF),
        in_specs=[
            whole((3, SEQ, 128)), whole((SEQ, 1)), pl.BlockSpec((1, QB), lambda i: (0, i)),
            pl.BlockSpec((1, QB, 128), lambda i: (0, i, 0)), pl.BlockSpec((1, QB, 128), lambda i: (0, i, 0)),
            pl.BlockSpec((8, QB), lambda i: (0, i)),
        ],
        out_specs=whole((3, SEQ, 128)),
        scratch_shapes=[pltpu.VMEM((128, SEQ), BF), pltpu.VMEM((SEQ, 128), F32), pltpu.VMEM((SEQ, 128), F32)],
        compiler_params=pltpu.CompilerParams(vmem_limit_bytes=VMEM_LIMIT),
    )(x, kpos, qpos, x, do, lse)


def positions(block_order):
    index = jnp.arange(SEQ, dtype=jnp.int32)
    blocks = block_order.shape[0]
    length = SEQ // blocks
    table = jnp.arange(blocks, dtype=jnp.int32)
    chosen = jnp.sum(jnp.where((index // length)[:, None] == table[None, :], block_order[None, :], 0), axis=1)
    return chosen * length + index % length


def packed(chunk, qkv, out, fc, gains, biases, fc_bias):
    wide_rows = lax.dynamic_update_slice(
        jnp.zeros((8, WIDTH), BF), jnp.concatenate([gains, biases], 0), (0, 12 * chunk))
    gain0, gain1 = wide_rows[0:1], wide_rows[1:2]
    bias = [wide_rows[2 + i:3 + i] for i in range(6)]
    none = jnp.zeros((1, WIDTH), BF)
    fc_rows = lax.dynamic_update_slice(jnp.zeros((FF,), BF), fc_bias, (48 * chunk,)).reshape(4, WIDTH)
    a = jnp.concatenate([
        qkv[:, :WIDTH], bias[1], gain0, bias[0], none,
        qkv[:, WIDTH:2 * WIDTH], none, none, none, none,
        qkv[:, 2 * WIDTH:], bias[2], none, none, none,
        out, bias[3], gain1, bias[4], bias[5],
    ], 0)
    rows = []
    for k in range(4):
        rows += [fc[:, k * WIDTH:(k + 1) * WIDTH], fc_rows[k:k + 1], none, none, none]
    return a, jnp.concatenate(rows, 0)


def local(boundary, block_order, qkv_weight, out_weight, fc_weight, proj_weight, gains, biases, fc_bias):
    section = lax.axis_index("section")
    chunk = lax.axis_index("fsdp") * 16 + lax.axis_index("ctx")
    key_pos = positions(block_order)
    kpos, qpos = key_pos[:, None], key_pos[None, :]
    source = lax.broadcasted_iota(jnp.int32, (WIDTH, PADDED), 0)
    target = lax.broadcasted_iota(jnp.int32, (WIDTH, PADDED), 1)
    spread = ((target // 16 == source // 12) & (target % 16 == source % 12)).astype(BF)

    a, b = packed(chunk, qkv_weight[0], out_weight[0], fc_weight[0], gains[0], biases[0], fc_bias[0])
    ga, gb, gc = gather_all(a, b, proj_weight[0], False)
    ga, gb, gc = ga.reshape(64, 64, WIDTH), gb.reshape(64, 64, WIDTH), gc.reshape(FF, WIDTH)

    def forward(u):
        x = to_heads(qkv_call(u, ga, spread), 2)
        attended, lse = attend_call(x, kpos, qpos)
        o = from_heads(attended, UNITS, 3)
        y, r, f = mlp_call(o, u, ga, gb, gc, spread)
        return y, (u, x, lse, o, r, f)

    def backward(full, saved, g):
        u, x, lse, o, r, f = saved
        do, dr, *more = mlp_back_call(full, g, f, r, ga, gb, gc, spread)
        dx = from_heads(attend_back_call(x, kpos, qpos, to_heads(do, 4), lse), UNITS, 5)
        if not full:
            return qkv_back_call(False, dx, ga, u, dr, spread)[0]
        small, grad_b, grad_c = more
        gu, grad_a = qkv_back_call(True, dx, ga, u, dr, spread, o, small)
        return gu, grad_a, grad_b, grad_c

    held = boundary[0].reshape(ROWS, WIDTH)
    first, _ = forward(held)
    sent = lax.ppermute(first.astype(BF), "section", [(0, 1)])
    y, saved = forward(jnp.where(section == 0, held, sent))
    back = backward(False, saved, held)
    returned = lax.ppermute(back.astype(BF), "section", [(1, 0)])
    gu, grad_a, grad_b, grad_c = backward(True, saved, jnp.where(section == 1, held, returned))
    ends = jnp.where(section == 0, gu, y).reshape(1, 2, 1, 64, WIDTH)
    ra, rb, rc = scatter_all(
        grad_a.reshape(4, 4, 4, 64, WIDTH), grad_b.reshape(4, 4, 4, 64, WIDTH), grad_c.reshape(4, 4, 4, 48, WIDTH))
    qkv_grad = jnp.concatenate([ra[0:12], ra[16:28], ra[32:44]], 1)
    fc_grad = jnp.concatenate([rb[16 * k:16 * k + 12] for k in range(4)], 1)
    small = jnp.stack([ra[61], ra[13], ra[62], ra[12], ra[44], ra[60], ra[14], ra[15]])
    small = lax.dynamic_slice(small, (0, 12 * chunk), (8, 12))
    fc_rows = jnp.concatenate([rb[16 * k + 12] for k in range(4)])
    fc_small = lax.dynamic_slice(fc_rows, (48 * chunk,), (48,))
    return (
        ends, qkv_grad[None], ra[48:60][None], fc_grad[None], rc[None],
        small[0:2][None], small[2:8][None], fc_small[None],
    )


def solution(mesh):
    rows = P("section", ("fsdp", "ctx"), None)
    lanes = P("section", None, ("fsdp", "ctx"))
    ends = P("section", None, "fsdp", "ctx", None)
    flat_rows = P("section", ("fsdp", "ctx"))
    return jax.shard_map(
        local, mesh=mesh,
        in_specs=(ends, P(), rows, rows, rows, rows, lanes, lanes, flat_rows),
        out_specs=(ends, rows, rows, rows, rows, lanes, lanes, flat_rows),
        check_vma=False)
```

time: 2230 us -> 425 us (0.19)
  blocking collectives: 1170 us -> 0 us
  waiting for transfers between devices: 482 us -> 2.85 us
  Pallas kernels: 0 us -> 379 us
  local copies, waits for them, and re-layouts: 192 us -> 27.5 us
  matrix products: 152 us -> 0 us
  starting transfers between devices: 151 us -> 2.81 us
  other arithmetic: 38.7 us -> 10.2 us
    unnamed x3 -> x0, blocking collectives: 818 us -> none
    pallas_call x0 -> x22, Pallas kernels: none -> 379 us  [the longest x1 87.1 us: gather_all(): pl.pallas_call(functools.partial(gather_kernel, priority), out_shape=[jax...]
    all_gather x2 -> x0, blocking collectives: 353 us -> none  [the longest x1 181 us: collect(): lax.all_gather(biases[0], ('fsdp', 'ctx'), axis=1, tiled=True)]
    reduce_scatter x7 -> x0, waiting for transfers between devices: 311 us -> none  [the longest x3 192 us: backward(): lax.psum_scatter(part_keys.astype(jnp.bfloat16), 'ctx', scatter_dimension...]
    all_gather x10 -> x0, waiting for transfers between devices: 160 us -> none  [the longest x3 81.6 us: forward(): lax.all_gather(value_rows, 'ctx', axis=1, tiled=True)]
    dot_general x54 -> x0, matrix products: 152 us -> none  [the longest x3 24.1 us: backward(): jnp.einsum('snd,snf->df', second, grad_pre, preferred_element_type=jnp.fl...]
    unnamed x48 -> x0, starting transfers between devices: 144 us -> none
    unnamed x407 -> x15, local copies, waits for them, and re-layouts: 102 us -> 3.49 us
  transfers between devices with their start and end apart: 69 -> 2, of which waited for: 16 -> 2; matrix products, arithmetic and copies ran while one was open for 26% -> 0% of each run, Pallas kernels for 0% -> 0%
where the time goes in v1:
time: 425 us; the launch traced here: 423 us
  Pallas kernels  379 us (89%)
  local copies, waits for them, and re-layouts  27.5 us (6%)
  other arithmetic  10.2 us (2%)
    pallas_call x1, Pallas kernels, gather_all(): pl.pallas_call(functools.partial(gather_kernel, priority), out_shape=[jax...  87.1 us
    pallas_call x1, Pallas kernels, scatter_all(): pl.pallas_call(scatter_kernel, out_shape=[jax.ShapeDtypeStruct((r, 768),...  81.1 us
    pallas_call x4, Pallas kernels, to_heads(): pl.pallas_call(functools.partial(to_heads_kernel, units), out_shape=jax.S...  47.6 us
    pallas_call x4, Pallas kernels, from_heads(): pl.pallas_call(functools.partial(from_heads_kernel, units), out_shape=jax...  45 us
    pallas_call x2, Pallas kernels, mlp_back_call(): pl.pallas_call(functools.partial(mlp_back_kernel, full), grid=(4,), out_s...  29.4 us
    pallas_call x2, Pallas kernels, attend_back_call(): pl.pallas_call(attend_back_kernel, grid=(SEQ // QB,), out_shape=jax.Shape...  20.7 us
    pallas_call x2, Pallas kernels, attend_call(): pl.pallas_call(attend_kernel, grid=(SEQ // QB,), out_shape=[jax.ShapeDtyp...  19.2 us
    pallas_call x2, Pallas kernels, mlp_call(): pl.pallas_call(mlp_kernel, grid=(4,), out_shape=[jax.ShapeDtypeStruct((RO...  18.8 us
  transfers between devices with their start and end apart: 2, of which 2 were waited for; matrix products, arithmetic and copies ran while one was open for 0% of the time, Pallas kernels for 0%

profile of v1, /device:TPU:0, one launch (start us, length us, event | category | flops | bytes accessed | tf_op | source)
XLA Modules:
  0.0 423.5 jit_solution(8874074794344589371)
XLA Ops:
  0.7 0.7 pad_maximum_fusion
  1.4 0.2 dynamic_update_slice.6
  1.6 0.7 select_reduce_fusion
  2.4 0.6 fusion.16.qpos_ref
  3.0 0.8 dynamic_update_slice.7
  3.9 0.8 fusion.28
  4.7 0.8 fusion.27
  5.5 0.2 copy.28
  5.7 0.9 fusion.2.kpos_ref
  6.6 7.7 %concatenate.24.b_ref = bf16[64,768]{1,0:T(8,128)(2,1)} concatenate(bf16[12,768]{1,0:T(8,128)(2,1)S(1)} %get-tuple-element.97, bf16[1,768]{1,0:T(2,128)(2,1)S(1)} %slice.145, bf16[3,768]{1,0:T(4,128)(2,1)S(1)} %broadcast.179, bf16[12,768]{1,0:T(8,128)(2,1)S(1)} %get-tuple-element.96, bf16[1,768]{1,0:T(2,128)(2,1)S(1)} %slice.148, bf16[3,768]{1,0:T(4,128)(2,1)S(1)} %broadcast.179, ...), dimensions={0} | concatenate | bytes 196608 | tf_op jit(solution)/shard_map/concatenate | solution.py:832
  14.3 8.5 %concatenate.23.a_ref = bf16[64,768]{1,0:T(8,128)(2,1)} concatenate(bf16[12,768]{1,0:T(8,128)(2,1)S(1)} %get-tuple-element.100, bf16[1,768]{1,0:T(2,128)(2,1)S(1)} %get-tuple-element.106, bf16[1,768]{1,0:T(2,128)(2,1)S(1)} %get-tuple-element.105, bf16[1,768]{1,0:T(2,128)(2,1)S(1)} %get-tuple-element.104, bf16[1,768]{1,0:T(2,128)(2,1)S(1)} %broadcast_in_dim.48, ...), dimensions={0} | concatenate | bytes 196608 | tf_op jit(solution)/shard_map/concatenate | solution.py:823
  22.8 87.1 %shard_map.152 = (bf16[4,4,4,64,768]{4,3,2,1,0:T(8,128)(2,1)}, bf16[4,4,4,64,768]{4,3,2,1,0:T(8,128)(2,1)}, bf16[4,4,4,48,768]{4,3,2,1,0:T(8,128)(2,1)}) custom-call(bf16[64,768]{1,0:T(8,128)(2,1)} %concatenate.23.a_ref, bf16[64,768]{1,0:T(8,128)(2,1)} %concatenate.24.b_ref, bf16[48,768]{1,0:T(8,128)(2,1)} %bitcast.60), custom_call_target="tpu_custom_call" | custom-call | tf_op jit(solution)/shard_map/pallas_call | solution.py:117
  109.9 2.3 fusion.1.e_ref
  112.2 6.0 %shard_map.153.x_ref = bf16[12,3,64,128]{3,2,1,0:T(8,128)(2,1)} custom-call(bf16[128,768]{1,0:T(8,128)(2,1)} %bitcast.52, bf16[64,64,768]{2,1,0:T(8,128)(2,1)} %bitcast.34, bf16[768,1024]{1,0:T(8,128)(2,1)} %fusion.1.e_ref), custom_call_target="tpu_custom_call" | custom-call | tf_op jit(solution)/shard_map/pallas_call | solution.py:511
  118.2 10.8 %shard_map.154.x_ref.q_ref = bf16[3,1024,128]{2,1,0:T(8,128)(2,1)} custom-call(bf16[12,3,64,128]{3,2,1,0:T(8,128)(2,1)} %shard_map.153.x_ref), custom_call_target="tpu_custom_call" | custom-call | tf_op jit(solution)/shard_map/pallas_call | solution.py:353
  129.0 9.6 %shard_map.155 = (bf16[1,1024,128]{2,1,0:T(8,128)(2,1)}, f32[8,1024]{1,0:T(8,128)}) custom-call(bf16[3,1024,128]{2,1,0:T(8,128)(2,1)} %shard_map.154.x_ref.q_ref, s32[1024,1]{1,0:T(8,128)} %fusion.2.kpos_ref, s32[1,1024]{1,0:T(1,128)} %fusion.16.qpos_ref, bf16[3,1024,128]{2,1,0:T(8,128)(2,1)} %shard_map.154.x_ref.q_ref), custom_call_target="tpu_custom_call" | custom-call | tf_op jit(solution)/shard_map/pallas_call | solution.py:745
  138.6 9.7 %shard_map.156.o_ref = bf16[12,1,64,128]{3,2,1,0:T(8,128)(2,1)} custom-call(bf16[1,1024,128]{2,1,0:T(8,128)(2,1)} %get-tuple-element.31.y_ref), custom_call_target="tpu_custom_call" | custom-call | tf_op jit(solution)/shard_map/pallas_call | solution.py:411
  148.4 0.0 copy-start
  148.4 9.4 %shard_map.157 = (f32[128,768]{1,0:T(8,128)}, f32[128,768]{1,0:T(8,128)}, f32[128,3072]{1,0:T(8,128)}) custom-call(bf16[12,1,64,128]{3,2,1,0:T(8,128)(2,1)} %shard_map.156.o_ref, bf16[128,768]{1,0:T(8,128)(2,1)} %bitcast.53, bf16[64,64,768]{2,1,0:T(8,128)(2,1)} %bitcast.35, bf16[64,64,768]{2,1,0:T(8,128)(2,1)} %bitcast.42, bf16[3072,768]{1,0:T(8,128)(2,1)} %bitcast.46, ...), custom_call_target="tpu_custom_call" | custom-call | tf_op jit(solution)/shard_map/pallas_call | solution.py:545
  157.8 1.0 convert_element_type.24
  158.8 1.3 collective-permute-start
  160.1 1.0 collective-permute-done
  161.2 0.0 copy-done
  161.2 0.7 broadcast_select_fusion.2.u_ref
  161.9 6.0 %shard_map.158.x_ref = bf16[12,3,64,128]{3,2,1,0:T(8,128)(2,1)} custom-call(bf16[128,768]{1,0:T(8,128)(2,1)} %broadcast_select_fusion.2.u_ref, bf16[64,64,768]{2,1,0:T(8,128)(2,1)} %bitcast.36, bf16[768,1024]{1,0:T(8,128)(2,1)} %fusion.1.e_ref), custom_call_target="tpu_custom_call" | custom-call | tf_op jit(solution)/shard_map/pallas_call | solution.py:511
  167.9 15.7 %shard_map.159.x_ref.q_ref = bf16[3,1024,128]{2,1,0:T(8,128)(2,1)} custom-call(bf16[12,3,64,128]{3,2,1,0:T(8,128)(2,1)} %shard_map.158.x_ref), custom_call_target="tpu_custom_call" | custom-call | tf_op jit(solution)/shard_map/pallas_call | solution.py:353
  183.5 9.6 %shard_map.160 = (bf16[1,1024,128]{2,1,0:T(8,128)(2,1)}, f32[8,1024]{1,0:T(8,128)}) custom-call(bf16[3,1024,128]{2,1,0:T(8,128)(2,1)} %shard_map.159.x_ref.q_ref, s32[1024,1]{1,0:T(8,128)} %fusion.2.kpos_ref, s32[1,1024]{1,0:T(1,128)} %fusion.16.qpos_ref, bf16[3,1024,128]{2,1,0:T(8,128)(2,1)} %shard_map.159.x_ref.q_ref), custom_call_target="tpu_custom_call" | custom-call | tf_op jit(solution)/shard_map/pallas_call | solution.py:745
  193.2 10.9 %shard_map.161.o_ref.refs_0_ = bf16[12,1,64,128]{3,2,1,0:T(8,128)(2,1)} custom-call(bf16[1,1024,128]{2,1,0:T(8,128)(2,1)} %get-tuple-element.35.y_ref), custom_call_target="tpu_custom_call" | custom-call | tf_op jit(solution)/shard_map/pallas_call | solution.py:411
  204.1 9.4 %shard_map.162 = (f32[128,768]{1,0:T(8,128)}, f32[128,768]{1,0:T(8,128)}, f32[128,3072]{1,0:T(8,128)}) custom-call(bf16[12,1,64,128]{3,2,1,0:T(8,128)(2,1)} %shard_map.161.o_ref.refs_0_, bf16[128,768]{1,0:T(8,128)(2,1)} %broadcast_select_fusion.2.u_ref, bf16[64,64,768]{2,1,0:T(8,128)(2,1)} %bitcast.37, bf16[64,64,768]{2,1,0:T(8,128)(2,1)} %bitcast.43, ...), custom_call_target="tpu_custom_call" | custom-call | tf_op jit(solution)/shard_map/pallas_call | solution.py:545
  213.5 12.3 %shard_map.163 = (bf16[12,1,64,128]{3,2,1,0:T(8,128)(2,1)}, f32[128,768]{1,0:T(8,128)}) custom-call(bf16[128,768]{1,0:T(8,128)(2,1)} %bitcast.54, f32[128,3072]{1,0:T(8,128)} %get-tuple-element.36.f_ref, f32[128,768]{1,0:T(8,128)} %get-tuple-element.37.r_ref, bf16[64,64,768]{2,1,0:T(8,128)(2,1)} %bitcast.38, bf16[64,64,768]{2,1,0:T(8,128)(2,1)} %bitcast.44, ...), custom_call_target="tpu_custom_call" | custom-call | tf_op jit(solution)/shard_map/pallas_call | solution.py:618
  225.7 9.8 %shard_map.164.do_ref = bf16[1,1024,128]{2,1,0:T(8,128)(2,1)} custom-call(bf16[12,1,64,128]{3,2,1,0:T(8,128)(2,1)} %get-tuple-element.38.x_ref), custom_call_target="tpu_custom_call" | custom-call | tf_op jit(solution)/shard_map/pallas_call | solution.py:353
  235.5 10.4 %shard_map.165.y_ref = bf16[3,1024,128]{2,1,0:T(8,128)(2,1)} custom-call(bf16[3,1024,128]{2,1,0:T(8,128)(2,1)} %shard_map.159.x_ref.q_ref, s32[1024,1]{1,0:T(8,128)} %fusion.2.kpos_ref, s32[1,1024]{1,0:T(1,128)} %fusion.16.qpos_ref, bf16[3,1024,128]{2,1,0:T(8,128)(2,1)} %shard_map.159.x_ref.q_ref, bf16[1,1024,128]{2,1,0:T(8,128)(2,1)} %shard_map.164.do_ref, ...), custom_call_target="tpu_custom_call" | custom-call | tf_op jit(solution)/shard_map/pallas_call | solution.py:792
  245.9 10.9 %shard_map.166.dx_ref = bf16[12,3,64,128]{3,2,1,0:T(8,128)(2,1)} custom-call(bf16[3,1024,128]{2,1,0:T(8,128)(2,1)} %shard_map.165.y_ref), custom_call_target="tpu_custom_call" | custom-call | tf_op jit(solution)/shard_map/pallas_call | solution.py:411
  256.7 0.0 copy-start.1
  256.8 7.5 %shard_map.167 = f32[128,768]{1,0:T(8,128)} custom-call(bf16[12,3,64,128]{3,2,1,0:T(8,128)(2,1)} %shard_map.166.dx_ref, bf16[64,64,768]{2,1,0:T(8,128)(2,1)} %bitcast.39, bf16[128,768]{1,0:T(8,128)(2,1)} %broadcast_select_fusion.2.u_ref, f32[128,768]{1,0:T(8,128)} %get-tuple-element.40.dr_ref, bf16[768,1024]{1,0:T(8,128)(2,1)} %fusion.1.e_ref), custom_call_target="tpu_custom_call" | custom-call | tf_op jit(solution)/shard_map/pallas_call | solution.py:701
  264.2 1.0 convert_element_type.25
  265.2 1.5 collective-permute-start.1
  266.8 1.8 collective-permute-done.1
  268.6 0.0 copy-done.1
  268.6 0.7 broadcast_select_fusion.g_ref
  269.3 17.1 %shard_map.168 = (bf16[12,1,64,128]{3,2,1,0:T(8,128)(2,1)}, f32[128,768]{1,0:T(8,128)}, f32[8,768]{1,0:T(8,128)}, bf16[64,64,768]{2,1,0:T(8,128)(2,1)}, bf16[3072,768]{1,0:T(8,128)(2,1)}) custom-call(bf16[128,768]{1,0:T(8,128)(2,1)} %broadcast_select_fusion.g_ref, f32[128,3072]{1,0:T(8,128)} %get-tuple-element.36.f_ref, f32[128,768]{1,0:T(8,128)} %get-tuple-element.37.r_ref, ...), custom_call_target="tpu_custom_call" | custom-call | tf_op jit(solution)/shard_map/pallas_call | solution.py:618
  286.4 11.4 %shard_map.169.do_ref = bf16[1,1024,128]{2,1,0:T(8,128)(2,1)} custom-call(bf16[12,1,64,128]{3,2,1,0:T(8,128)(2,1)} %get-tuple-element.41.x_ref), custom_call_target="tpu_custom_call" | custom-call | tf_op jit(solution)/shard_map/pallas_call | solution.py:353
  297.8 10.4 %shard_map.170.y_ref = bf16[3,1024,128]{2,1,0:T(8,128)(2,1)} custom-call(bf16[3,1024,128]{2,1,0:T(8,128)(2,1)} %shard_map.159.x_ref.q_ref, s32[1024,1]{1,0:T(8,128)} %fusion.2.kpos_ref, s32[1,1024]{1,0:T(1,128)} %fusion.16.qpos_ref, bf16[3,1024,128]{2,1,0:T(8,128)(2,1)} %shard_map.159.x_ref.q_ref, bf16[1,1024,128]{2,1,0:T(8,128)(2,1)} %shard_map.169.do_ref, ...), custom_call_target="tpu_custom_call" | custom-call | tf_op jit(solution)/shard_map/pallas_call | solution.py:792
  308.2 13.4 %shard_map.171.dx_ref = bf16[12,3,64,128]{3,2,1,0:T(8,128)(2,1)} custom-call(bf16[3,1024,128]{2,1,0:T(8,128)(2,1)} %shard_map.170.y_ref), custom_call_target="tpu_custom_call" | custom-call | tf_op jit(solution)/shard_map/pallas_call | solution.py:411
  321.6 10.8 %shard_map.172 = (f32[128,768]{1,0:T(8,128)}, bf16[64,64,768]{2,1,0:T(8,128)(2,1)}) custom-call(bf16[12,3,64,128]{3,2,1,0:T(8,128)(2,1)} %shard_map.171.dx_ref, bf16[64,64,768]{2,1,0:T(8,128)(2,1)} %bitcast.41, bf16[128,768]{1,0:T(8,128)(2,1)} %broadcast_select_fusion.2.u_ref, f32[128,768]{1,0:T(8,128)} %get-tuple-element.42.dr_ref, ...), custom_call_target="tpu_custom_call" | custom-call | tf_op jit(solution)/shard_map/pallas_call | solution.py:701
  332.5 81.1 %shard_map.173 = (f32[64,768]{1,0:T(8,128)}, f32[64,768]{1,0:T(8,128)}, f32[48,768]{1,0:T(8,128)}) custom-call(bf16[4,4,4,64,768]{4,3,2,1,0:T(8,128)(2,1)} %bitcast.51, bf16[4,4,4,64,768]{4,3,2,1,0:T(8,128)(2,1)} %bitcast.50, bf16[4,4,4,48,768]{4,3,2,1,0:T(8,128)(2,1)} %bitcast.55), custom_call_target="tpu_custom_call" | custom-call | tf_op jit(solution)/shard_map/pallas_call | solution.py:288
  413.6 0.0 copy-start.4
  413.6 0.9 slice_reduce_fusion.3
  414.5 0.9 fusion.26
  415.4 0.7 slice.169
  416.1 0.9 fusion.25
  417.0 0.9 slice_bitcast_fusion
  417.9 0.1 constant_dynamic-slice_fusion
  418.0 0.6 slice_bitcast_fusion.2
  418.6 0.8 copy.32
  419.4 0.7 copy.31
  420.1 0.6 copy.33
  420.6 0.8 copy.30
  421.4 0.0 copy-done.2
  421.4 0.0 copy-done.3
  421.4 0.8 broadcast_select_fusion.1
  422.2 0.6 fusion.24
  422.8 0.0 copy-done.4
  422.8 0.7 copy.37
  (26 shorter events, 0.2 us)
Async XLA Ops:
  148.4 12.8 %copy-start = (bf16[1,2,1,64,768]{4,3,2,1,0:T(8,128)(2,1)S(1)}, bf16[1,2,1,64,768]{4,3,2,1,0:T(8,128)(2,1)}, u32[]{:S(2)}) copy-start(bf16[1,2,1,64,768]{4,3,2,1,0:T(8,128)(2,1)} %param.9) | copy-start | bytes 589828
  158.8 2.4 collective-permute-start
  256.7 11.8 %copy-start.1 = (bf16[1,2,1,64,768]{4,3,2,1,0:T(8,128)(2,1)S(1)}, bf16[1,2,1,64,768]{4,3,2,1,0:T(8,128)(2,1)}, u32[]{:S(2)}) copy-start(bf16[1,2,1,64,768]{4,3,2,1,0:T(8,128)(2,1)} %param.9) | copy-start | bytes 589828
  265.2 3.3 collective-permute-start.1
  332.4 89.0 %copy-start.2 = (f32[128,768]{1,0:T(8,128)S(1)}, f32[128,768]{1,0:T(8,128)}, u32[]{:S(2)}) copy-start(f32[128,768]{1,0:T(8,128)} %get-tuple-element.45) | copy-start | bytes 1179652
  332.4 89.0 %copy-start.3 = (f32[128,768]{1,0:T(8,128)S(1)}, f32[128,768]{1,0:T(8,128)}, u32[]{:S(2)}) copy-start(f32[128,768]{1,0:T(8,128)} %get-tuple-element.44) | copy-start | bytes 1179652
  413.6 9.2 %copy-start.4 = (f32[48,768]{1,0:T(8,128)S(1)}, f32[48,768]{1,0:T(8,128)}, u32[]{:S(2)}) copy-start(f32[48,768]{1,0:T(8,128)} %get-tuple-element.51) | copy-start | bytes 442372
